TPU v7x, 1024 devices: a whole 4x8x16 slice. The times are simulated.
1024 devices in a mesh: sec: 4 (over z_hi), patch: 32 (over y, x), lev: 8 (over z_lo, core).
Axes of the slice: x: 4, y: 8, z: 16 (z_hi: 4, z_lo: 4; z = z_hi * 4 + z_lo), core: 2. Of those that a mesh axis runs over, the one named last changes fastest.
Arguments:
- atm_tracers: float32 [10, 128, 262144], P(None, 'lev', ('sec', 'patch')), may hold values from -6 to 6
- neighbor_offsets: int32 [3, 262144], P(None, ('sec', 'patch')), may hold values from -2 to 2
- edge_weights: float32 [3, 262144], P(None, ('sec', 'patch')), may hold values from 0.03 to 0.15
- vertical_rates: float32 [10], replicated, may hold values from 0.03 to 0.15
- flux_mixing: float32 [10, 10], replicated, may hold values from -16 to 16
- owners: int32 [262144, 1], P(('sec', 'patch', 'lev')), may hold values from 0 to 31; in each aligned block of 256 rows (0 to 255, 256 to 511, ...) at most 16 rows name the same one
- remap_weights: bfloat16 [512, 262144], P(None, ('sec', 'patch', 'lev')), may hold values from -0.375 to 0.375
- ocean_mask: int32 [262144], P(('sec', 'patch', 'lev')), may hold values 0 or 1
- ocean_state: float32 [2, 80, 262144], P(None, None, ('sec', 'patch', 'lev')), may hold values from -6 to 6
- forcing_mixing: float32 [2, 10], replicated, may hold values from -4 to 4
Outputs:
- atm_out: float32 [10, 128, 262144], P(None, 'lev', ('sec', 'patch'))
- marine_successor_fields: float32 [2, 80, 262144], P(None, None, ('sec', 'patch', 'lev'))
- atm_surface: float32 [262144], P(('sec', 'patch', 'lev'))
Inputs may be any that keep to these rules, and one draw needn't show every extreme that they name: `owners`: within the columns of one device, no owner is named by more than 16 columns, a bound that some block reaches.
All inputs are finite; a program needn't handle non-finite values. No bound on the sum of `ocean_mask` on one device may be relied on, other than what follows from the above.
Results may differ from a plain program's by a relative error of at most 0.00035.
Values sent between devices are 32-bit elements; how exact they have to be, the bound alone decides.
A program may use at most 32 MiB of HBM per device.

v0:
```python
import jax
import jax.numpy as jnp
from jax import lax
from jax.sharding import PartitionSpec as P

ALEV = 128
OLEV = 80


def extended_2(cells, sides, width):
    for axis, dim in sides:
        count = lax.axis_size(axis)
        head = lax.slice_in_dim(cells, 0, width, axis=dim)
        tail = lax.slice_in_dim(cells, cells.shape[dim] - width, cells.shape[dim], axis=dim)
        cells = jnp.concatenate(
            [
                lax.ppermute(tail, axis, [(i, (i + 1) % count) for i in range(count)]),
                cells,
                lax.ppermute(head, axis, [((i + 1) % count, i) for i in range(count)]),
            ],
            axis=dim,
        )
    return cells


def atm_step(q, offsets, edge_weights, vertical_rates, level_start):
    levels_here = q.shape[1]
    ncol = q.shape[2]
    extended = extended_2(q, ((("sec", "patch"), 2), ("lev", 1)), 2)
    col_ext = extended[:, 2:-2, :]
    lev_ext = extended[:, :, 2:-2]
    shifted = [col_ext[:, :, 2 + delta : 2 + delta + ncol] for delta in (-2, -1, 0, 1, 2)]
    result = q
    for j in range(3):
        neighbor = jnp.zeros_like(q)
        for position, delta in enumerate((-2, -1, 0, 1, 2)):
            picked = (offsets[j] == delta).astype(jnp.float32)[None, None, :]
            neighbor = neighbor + picked * shifted[position]
        result = result + edge_weights[j][None, None, :] * (neighbor - q)
    levels = level_start + jnp.arange(levels_here, dtype=jnp.int32)
    for m in (-2, -1, 1, 2):
        beside = lev_ext[:, 2 + m : 2 + m + levels_here, :]
        valid = ((levels + m >= 0) & (levels + m < ALEV)).astype(jnp.float32)
        factor = 1.0 if abs(m) == 1 else 0.5
        result = (
            result + (vertical_rates * factor)[:, None, None] * (beside - q) * valid[None, :, None]
        )
    return result


def ocean_step(state, forcing):
    levels = jnp.arange(OLEV, dtype=jnp.int32)
    profile = jnp.exp(-levels.astype(jnp.float32) / 8.0)
    result = state + profile[None, :, None] * forcing[:, None, :]
    for m in (-1, 1):
        beside = jnp.roll(state, -m, axis=1)
        valid = ((levels + m >= 0) & (levels + m < OLEV)).astype(jnp.float32)
        result = result + 0.2 * (beside - state) * valid[None, :, None]
    return result


def per_device(
    atm_tracers,
    neighbor_offsets,
    edge_weights,
    vertical_rates,
    flux_mixing,
    owners,
    remap_weights,
    ocean_mask,
    ocean_state,
    forcing_mixing,
):
    finest_arithmetic_mode = lax.Precision.HIGHEST
    patch_groups = lax.axis_size("patch")
    slot_capacity = remap_weights.shape[0] // patch_groups
    nflux = flux_mixing.shape[0]
    level_start = lax.axis_index("lev") * atm_tracers.shape[1]
    q = atm_tracers
    for step in range(2):
        q = atm_step(q, neighbor_offsets, edge_weights, vertical_rates, level_start)
    partial_sums = jnp.sum(q, axis=1)
    colmean = lax.psum_scatter(partial_sums, "lev", scatter_dimension=1, tiled=True) / ALEV
    flux = jnp.tanh(jnp.dot(flux_mixing, colmean, precision=finest_arithmetic_mode))
    owned = owners[:, 0]
    onehot = (owned[:, None] == jnp.arange(patch_groups, dtype=jnp.int32)[None, :]).astype(
        jnp.int32
    )
    rank = jnp.cumsum(onehot, axis=0) - onehot
    slot = jnp.sum(rank * onehot, axis=1)
    outgoing = (
        jnp.zeros((patch_groups, slot_capacity, nflux), jnp.float32)
        .at[owned, slot]
        .set(jnp.transpose(flux))
    )
    incoming = lax.all_to_all(outgoing, "patch", split_axis=0, concat_axis=0, tiled=True)
    regrid_operator = remap_weights.astype(jnp.float32)
    real_valued_filter = ocean_mask.astype(jnp.float32)
    oflux = (
        jnp.einsum(
            "sf,sc->fc",
            incoming.reshape(patch_groups * slot_capacity, nflux),
            regrid_operator,
            precision=finest_arithmetic_mode,
        )
        * real_valued_filter[None, :]
    )
    forcing = jnp.dot(forcing_mixing, oflux, precision=finest_arithmetic_mode)
    marine_successor_fields = ocean_step(ocean_state, forcing)
    marine_skin_warmth = marine_successor_fields[0, 0, :] * real_valued_filter
    gathered_exchange_rates = jnp.dot(
        regrid_operator, marine_skin_warmth, precision=finest_arithmetic_mode
    ).reshape(patch_groups, slot_capacity)
    returned = lax.all_to_all(
        gathered_exchange_rates, "patch", split_axis=0, concat_axis=0, tiled=True
    )
    atm_surface = returned[owned, slot]
    return (q, marine_successor_fields, atm_surface)


def solution(mesh):
    in_specs = (
        P(None, "lev", ("sec", "patch")),
        P(None, ("sec", "patch")),
        P(None, ("sec", "patch")),
        P(),
        P(),
        P(("sec", "patch", "lev"), None),
        P(None, ("sec", "patch", "lev")),
        P(("sec", "patch", "lev")),
        P(None, None, ("sec", "patch", "lev")),
        P(),
    )
    out_specs = (
        P(None, "lev", ("sec", "patch")),
        P(None, None, ("sec", "patch", "lev")),
        P(("sec", "patch", "lev")),
    )
    return jax.shard_map(
        per_device, mesh=mesh, in_specs=in_specs, out_specs=out_specs, check_vma=False
    )
```

profile of v0, /device:TPU:2, one launch (start us, length us, event | category | flops | bytes accessed | tf_op | source)
XLA Modules:
  0.0 206.6 jit_solution(14312103465881141039)
XLA Ops:
  7.2 0.0 copy-start
  7.2 0.0 reduce-scatter.2.cloned.1.call-start
  7.2 1.7 fusion.74
  8.9 3.4 %collective-permute-start = (f32[10,16,2]{2,1,0:T(8,128)}, f32[10,16,2]{2,1,0:T(8,128)S(1)}, u32[]{:S(2)}, u32[]{:S(2)}) collective-permute-start(f32[10,16,2]{2,1,0:T(8,128)} %get-tuple-element.17), channel_id=1, source_target_pairs={{0,8},{8,16},{16,24},{24,32},{32,40},{40,48},{48,56},{56,64},{64,7... | collective-permute-start | bytes 3848 | tf_op jit(solution)/shard_map/ppermute | solution.py:17
  12.3 13.6 %collective-permute-start.1 = (f32[10,16,2]{2,1,0:T(8,128)}, f32[10,16,2]{2,1,0:T(8,128)}, u32[]{:S(2)}, u32[]{:S(2)}) collective-permute-start(f32[10,16,2]{2,1,0:T(8,128)} %get-tuple-element.16), channel_id=1, source_target_pairs={{8,0},{16,8},{24,16},{32,24},{40,32},{48,40},{56,48},{64,56},{72,6... | collective-permute-start | bytes 3848 | tf_op jit(solution)/shard_map/ppermute | solution.py:19
  25.9 0.0 copy-start.41
  25.9 0.0 copy-start.34
  26.0 0.0 copy-start.35
  26.0 0.0 copy-start.1
  26.0 1.5 constant_dynamic-update-slice_fusion.1
  27.5 0.5 broadcast_multiply_fusion
  28.1 0.7 compare_convert_fusion.14
  28.8 0.6 fusion.77
  29.5 1.3 fusion.63
  30.8 0.5 and_convert_fusion
  31.3 2.2 %concatenate.54 = f32[10,16,2052]{2,1,0:T(8,128)} concatenate(f32[10,16,2]{2,1,0:T(8,128)S(1)} %collective-permute-done, f32[10,16,2048]{2,1,0:T(8,128)S(1)} %copy-done.1, f32[10,16,2]{2,1,0:T(8,128)} %collective-permute-done.1), dimensions={2} | concatenate | bytes 2626560 | tf_op jit(solution)/shard_map/concatenate | solution.py:15
  33.7 0.0 copy-start.44
  33.7 1.5 fusion.72
  35.3 1.9 collective-permute-start.3
  37.2 2.4 %collective-permute-start.2 = (f32[10,2,2052]{2,0,1:T(8,128)S(1)}, f32[10,2,2052]{2,0,1:T(8,128)S(1)}, u32[]{:S(2)}, u32[]{:S(2)}) collective-permute-start(f32[10,2,2052]{2,0,1:T(8,128)S(1)} %copy.35), channel_id=1, source_target_pairs={{0,1},{1,2},{2,3},{3,4},{4,5},{5,6},{6,7},{7,0},{8,9},{9,10},{10,1... | collective-permute-start | bytes 492488 | tf_op jit(solution)/shard_map/ppermute | solution.py:17
  39.7 0.9 constant_dynamic-update-slice_fusion
  40.6 1.8 collective-permute-done.3
  42.4 0.1 copy.38
  42.5 4.4 %collective-permute-done.2 = f32[10,2,2052]{2,0,1:T(8,128)S(1)} collective-permute-done((f32[10,2,2052]{2,0,1:T(8,128)S(1)}, f32[10,2,2052]{2,0,1:T(8,128)S(1)}, u32[]{:S(2)}, u32[]{:S(2)}) %collective-permute-start.2) | collective-permute-done | bytes 164192 | tf_op jit(solution)/shard_map/ppermute | solution.py:17
  46.9 0.1 copy.36
  47.2 6.0 %fusion.20 = f32[10,16,2048]{2,1,0:T(8,128)S(1)} fusion(f32[10,16,2048]{2,1,0:T(8,128)S(1)} %copy-done.1, f32[10,16,2052]{2,1,0:T(8,128)S(1)} %copy-done.3, f32[10,2,2052]{2,1,0:T(2,128)S(1)} %copy.38, f32[10,2,2052]{2,1,0:T(2,128)S(1)} %copy.36, f32[10,16,2]{2,1,0:T(8,128)S(1)} %collective-permute-done, f32[10,16,2050]{2,1,0:T(8,128)} %copy-done.2, ...), kind=kLoop, calls=%fused_computation.36 | loop fusion | flops 19005440 | bytes 7033552 | tf_op jit(solution)/shard_map/add | solution.py:46
  53.3 0.1 fusion.73
  53.4 1.9 collective-permute-start.4
  55.3 14.1 %collective-permute-start.5 = (f32[10,16,2]{2,1,0:T(8,128)S(1)}, f32[10,16,2]{2,1,0:T(8,128)S(1)}, u32[]{:S(2)}, u32[]{:S(2)}) collective-permute-start(f32[10,16,2]{2,1,0:T(8,128)S(1)} %get-tuple-element.14), channel_id=1, source_target_pairs={{8,0},{16,8},{24,16},{32,24},{40,32},{48,40},{56,48},{64,56},{72,6... | collective-permute-start | bytes 3848 | tf_op jit(solution)/shard_map/ppermute | solution.py:19
  69.4 0.6 fusion.76
  70.0 0.6 reduce-window.6
  70.6 0.9 collective-permute-done.5
  71.5 1.5 concatenate.59
  73.1 1.5 fusion.71
  74.6 1.9 collective-permute-start.7
  76.6 2.4 %collective-permute-start.6 = (f32[10,2,2052]{2,0,1:T(8,128)S(1)}, f32[10,2,2052]{2,0,1:T(8,128)S(1)}, u32[]{:S(2)}, u32[]{:S(2)}) collective-permute-start(f32[10,2,2052]{2,0,1:T(8,128)S(1)} %copy.39), channel_id=1, source_target_pairs={{0,1},{1,2},{2,3},{3,4},{4,5},{5,6},{6,7},{7,0},{8,9},{9,10},{10,1... | collective-permute-start | bytes 492488 | tf_op jit(solution)/shard_map/ppermute | solution.py:17
  79.0 0.2 slice_reduce_fusion
  79.2 0.8 fusion.62
  80.0 1.8 collective-permute-done.7
  81.7 0.1 copy.42
  81.8 4.4 %collective-permute-done.6 = f32[10,2,2052]{2,0,1:T(8,128)S(1)} collective-permute-done((f32[10,2,2052]{2,0,1:T(8,128)S(1)}, f32[10,2,2052]{2,0,1:T(8,128)S(1)}, u32[]{:S(2)}, u32[]{:S(2)}) %collective-permute-start.6) | collective-permute-done | bytes 164192 | tf_op jit(solution)/shard_map/ppermute | solution.py:17
  86.2 0.1 copy.40
  86.5 9.2 %fusion.68 = (f32[10,2048]{1,0:T(8,128)}, f32[10,16,2048]{2,1,0:T(8,128)}) fusion(f32[16]{0:T(128)} %get-tuple-element.40, f32[10,16,2048]{2,1,0:T(8,128)S(1)} %fusion.20, f32[10,2,2052]{2,1,0:T(2,128)S(1)} %copy.42, f32[10,16,2052]{2,1,0:T(8,128)} %concatenate.59, f32[16]{0:T(128)} %get-tuple-element.41, f32[16]{0:T(128)} %copy-done.46, ...), kind=kLoop, calls=%fused_computation.133 | loop fusion | flops 19968000 | bytes 4495312 | tf_op jit(solution)/shard_map/reduce_sum | solution.py:82
  95.6 0.0 reduce-scatter.2.cloned.1.call-update
  95.7 53.7 %reduce-scatter.2.cloned.1.call-done = f32[10,256]{1,0:T(8,128)} async-done(((f32[10,2048]{1,0:T(8,128)}), f32[10,256]{1,0:T(8,128)}) %reduce-scatter.2.cloned.1.call-update) | async-done | bytes 10256 | tf_op jit(solution)/shard_map/reduce_scatter | solution.py:83
  149.4 0.9 convolution_tanh_fusion
  150.3 0.1 copy.44
  150.5 0.0 copy-start.48
  150.5 12.1 %scatter_fusion = f32[32,16,10]{2,1,0:T(8,128)S(1)} fusion(f32[32,16,10]{2,1,0:T(8,128)S(1)} %broadcast_in_dim.2, s32[256]{0:T(256)S(1)} %bitcast.58, f32[256,10]{1,0:T(8,128)S(1)} %copy.44), kind=kCustom, calls=%fused_computation.1 | custom fusion | bytes 32768 | tf_op jit(solution)/shard_map/scatter | solution.py:94
  162.6 0.8 reshape.284
  163.4 9.9 %all-to-all-start = ((f32[32,1,160]{2,1,0:T(1,128)}), f32[32,1,160]{2,1,0:T(1,128)S(1)}, u32[]{:S(2)}, u32[]{:S(2)}) async-start(f32[32,1,160]{2,1,0:T(1,128)} %reshape.284), calls=%async_computation.1 | async-start | bytes 65536 | tf_op jit(solution)/shard_map/all_to_all | solution.py:96
  173.4 8.6 %all-to-all-done = f32[32,1,160]{2,1,0:T(1,128)S(1)} async-done(((f32[32,1,160]{2,1,0:T(1,128)}), f32[32,1,160]{2,1,0:T(1,128)S(1)}, u32[]{:S(2)}, u32[]{:S(2)}) %all-to-all-start) | async-done | bytes 20512 | tf_op jit(solution)/shard_map/all_to_all | solution.py:96
  182.0 0.5 broadcast.396
  182.5 0.7 reduce.2
  183.3 0.2 reshape.285
  183.4 0.3 convolution_multiply_fusion
  183.8 0.1 convolution_bitcast_fusion
  183.9 0.0 copy-done.38
  184.0 0.1 fusion.58
  184.1 0.0 copy-start.5
  184.1 0.3 fusion.78
  184.4 0.1 all_to_all.12
  184.5 12.7 %all_to_all.17 = f32[32,1,16]{2,1,0:T(1,128)S(1)} all-to-all(f32[32,1,16]{2,1,0:T(1,128)S(1)} %bitcast.97), channel_id=1, replica_groups=mesh['sec'=4,'patch'=32,'lev'=8] {'patch'}, dimensions={0} | all-to-all | bytes 4096 | tf_op jit(solution)/shard_map/all_to_all | solution.py:114
  197.2 2.5 %gather_fusion = f32[256]{0:T(256)} fusion(f32[32,16]{1,0:T(8,128)S(1)} %bitcast.57, s32[256]{0:T(256)S(1)} %bitcast.59), kind=kCustom, calls=%fused_computation | custom fusion | bytes 4096 | tf_op jit(solution)/shard_map/gather | solution.py:117
  (107 shorter events, 0.4 us)
Async XLA Ops:
  7.2 176.3 %copy-start = (bf16[512,256]{1,0:T(8,128)(2,1)S(1)}, bf16[512,256]{1,0:T(8,128)(2,1)}, u32[]{:S(2)}) copy-start(bf16[512,256]{1,0:T(8,128)(2,1)} %param.16) | copy-start | bytes 786436
  7.2 142.3 %reduce-scatter.2.cloned.1.call-start = ((), (), s32[]{:S(2)}) async-start(), calls=%async_computation.3 | async-start | bytes 147456 | tf_op jit(solution)/shard_map/reduce_scatter | solution.py:83
  8.9 22.4 %collective-permute-start = (f32[10,16,2]{2,1,0:T(8,128)}, f32[10,16,2]{2,1,0:T(8,128)S(1)}, u32[]{:S(2)}, u32[]{:S(2)}) collective-permute-start(f32[10,16,2]{2,1,0:T(8,128)} %get-tuple-element.17), channel_id=1, source_target_pairs={{0,8},{8,16},{16,24},{24,32},{32,40},{40,48},{48,56},{56,64},{64,7... | collective-permute-start | bytes 3848 | tf_op jit(solution)/shard_map/ppermute | solution.py:17
  12.3 19.0 %collective-permute-start.1 = (f32[10,16,2]{2,1,0:T(8,128)}, f32[10,16,2]{2,1,0:T(8,128)}, u32[]{:S(2)}, u32[]{:S(2)}) collective-permute-start(f32[10,16,2]{2,1,0:T(8,128)} %get-tuple-element.16), channel_id=1, source_target_pairs={{8,0},{16,8},{24,16},{32,24},{40,32},{48,40},{56,48},{64,56},{72,6... | collective-permute-start | bytes 3848 | tf_op jit(solution)/shard_map/ppermute | solution.py:19
  25.9 1.6 copy-start.41
  25.9 2.1 %copy-start.34 = (s32[3,2048]{1,0:T(4,128)S(1)}, s32[3,2048]{1,0:T(4,128)}, u32[]{:S(2)}) copy-start(s32[3,2048]{1,0:T(4,128)} %param.11) | copy-start | bytes 73732
  26.0 2.9 %copy-start.35 = (f32[3,2048]{1,0:T(4,128)S(1)}, f32[3,2048]{1,0:T(4,128)}, u32[]{:S(2)}) copy-start(f32[3,2048]{1,0:T(4,128)} %param.12) | copy-start | bytes 73732
  26.0 3.5 %copy-start.4 = (f32[2,80,256]{2,1,0:T(8,128)S(1)}, f32[2,80,256]{2,1,0:T(8,128)}, u32[]{:S(2)}) copy-start(f32[2,80,256]{2,1,0:T(8,128)} %param.18) | copy-start | bytes 491524
  26.0 5.3 %copy-start.1 = (f32[10,16,2048]{2,1,0:T(8,128)S(1)}, f32[10,16,2048]{2,1,0:T(8,128)}, u32[]{:S(2)}) copy-start(f32[10,16,2048]{2,1,0:T(8,128)} %param.10) | copy-start | bytes 3932164
  33.5 13.5 %copy-start.3 = (f32[10,16,2052]{2,1,0:T(8,128)S(1)}, f32[10,16,2052]{2,1,0:T(8,128)}, u32[]{:S(2)}) copy-start(f32[10,16,2052]{2,1,0:T(8,128)} %concatenate.54) | copy-start | bytes 3939844
  33.5 13.5 %copy-start.7 = (f32[1,2048]{1,0:T(1,128)S(1)}, f32[1,2048]{1,0:T(1,128)}, u32[]{:S(2)}) copy-start(f32[1,2048]{1,0:T(1,128)} %get-tuple-element.27) | copy-start | bytes 24580
  33.5 13.5 %copy-start.9 = (f32[1,2048]{1,0:T(1,128)S(1)}, f32[1,2048]{1,0:T(1,128)}, u32[]{:S(2)}) copy-start(f32[1,2048]{1,0:T(1,128)} %get-tuple-element.28) | copy-start | bytes 24580
  33.5 13.5 %copy-start.11 = (f32[1,2048]{1,0:T(1,128)S(1)}, f32[1,2048]{1,0:T(1,128)}, u32[]{:S(2)}) copy-start(f32[1,2048]{1,0:T(1,128)} %get-tuple-element.29) | copy-start | bytes 24580
  33.5 13.5 %copy-start.13 = (f32[1,2048]{1,0:T(1,128)S(1)}, f32[1,2048]{1,0:T(1,128)}, u32[]{:S(2)}) copy-start(f32[1,2048]{1,0:T(1,128)} %get-tuple-element.30) | copy-start | bytes 24580
  33.5 13.5 %copy-start.15 = (f32[1,2048]{1,0:T(1,128)S(1)}, f32[1,2048]{1,0:T(1,128)}, u32[]{:S(2)}) copy-start(f32[1,2048]{1,0:T(1,128)} %get-tuple-element.31) | copy-start | bytes 24580
  33.6 13.5 %copy-start.17 = (f32[1,2048]{1,0:T(1,128)S(1)}, f32[1,2048]{1,0:T(1,128)}, u32[]{:S(2)}) copy-start(f32[1,2048]{1,0:T(1,128)} %get-tuple-element.32) | copy-start | bytes 24580
  33.6 13.5 %copy-start.19 = (f32[1,2048]{1,0:T(1,128)S(1)}, f32[1,2048]{1,0:T(1,128)}, u32[]{:S(2)}) copy-start(f32[1,2048]{1,0:T(1,128)} %get-tuple-element.33) | copy-start | bytes 24580
  33.6 13.5 %copy-start.21 = (f32[1,2048]{1,0:T(1,128)S(1)}, f32[1,2048]{1,0:T(1,128)}, u32[]{:S(2)}) copy-start(f32[1,2048]{1,0:T(1,128)} %get-tuple-element.34) | copy-start | bytes 24580
  33.6 13.5 %copy-start.23 = (f32[1,2048]{1,0:T(1,128)S(1)}, f32[1,2048]{1,0:T(1,128)}, u32[]{:S(2)}) copy-start(f32[1,2048]{1,0:T(1,128)} %get-tuple-element.35) | copy-start | bytes 24580
  33.6 13.5 %copy-start.25 = (f32[1,2048]{1,0:T(1,128)S(1)}, f32[1,2048]{1,0:T(1,128)}, u32[]{:S(2)}) copy-start(f32[1,2048]{1,0:T(1,128)} %get-tuple-element.36) | copy-start | bytes 24580
  33.6 13.5 %copy-start.27 = (f32[1,2048]{1,0:T(1,128)S(1)}, f32[1,2048]{1,0:T(1,128)}, u32[]{:S(2)}) copy-start(f32[1,2048]{1,0:T(1,128)} %get-tuple-element.37) | copy-start | bytes 24580
  33.6 13.5 %copy-start.29 = (f32[1,2048]{1,0:T(1,128)S(1)}, f32[1,2048]{1,0:T(1,128)}, u32[]{:S(2)}) copy-start(f32[1,2048]{1,0:T(1,128)} %get-tuple-element.38) | copy-start | bytes 24580
  33.6 13.5 %copy-start.30 = (f32[1,2048]{1,0:T(1,128)S(1)}, f32[1,2048]{1,0:T(1,128)}, u32[]{:S(2)}) copy-start(f32[1,2048]{1,0:T(1,128)} %get-tuple-element.39) | copy-start | bytes 24580
  33.6 13.5 %copy-start.31 = (f32[1,2048]{1,0:T(1,128)S(1)}, f32[1,2048]{1,0:T(1,128)}, u32[]{:S(2)}) copy-start(f32[1,2048]{1,0:T(1,128)} %get-tuple-element.22) | copy-start | bytes 24580
  33.6 13.5 %copy-start.32 = (f32[1,2048]{1,0:T(1,128)S(1)}, f32[1,2048]{1,0:T(1,128)}, u32[]{:S(2)}) copy-start(f32[1,2048]{1,0:T(1,128)} %get-tuple-element.23) | copy-start | bytes 24580
  33.7 13.5 %copy-start.33 = (f32[1,2048]{1,0:T(1,128)S(1)}, f32[1,2048]{1,0:T(1,128)}, u32[]{:S(2)}) copy-start(f32[1,2048]{1,0:T(1,128)} %get-tuple-element.24) | copy-start | bytes 24580
  33.7 13.5 %copy-start.42 = (f32[10]{0:T(128)S(1)}, f32[10]{0:T(128)}, u32[]{:S(2)}) copy-start(f32[10]{0:T(128)} %param.13) | copy-start | bytes 124
  33.7 13.5 %copy-start.43 = (f32[10]{0:T(128)S(1)}, f32[10]{0:T(128)}, u32[]{:S(2)}) copy-start(f32[10]{0:T(128)} %broadcast_multiply_fusion) | copy-start | bytes 124
  33.7 13.5 %copy-start.44 = (f32[16]{0:T(128)S(1)}, f32[16]{0:T(128)}, u32[]{:S(2)}) copy-start(f32[16]{0:T(128)} %get-tuple-element.40) | copy-start | bytes 196
  33.7 13.5 %copy-start.45 = (f32[16]{0:T(128)S(1)}, f32[16]{0:T(128)}, u32[]{:S(2)}) copy-start(f32[16]{0:T(128)} %get-tuple-element.41) | copy-start | bytes 196
  35.3 7.1 %collective-permute-start.3 = (f32[10,2,2052]{2,0,1:T(8,128)S(1)}, f32[10,2,2052]{2,0,1:T(8,128)S(1)}, u32[]{:S(2)}, u32[]{:S(2)}) collective-permute-start(f32[10,2,2052]{2,0,1:T(8,128)S(1)} %copy.37), channel_id=1, source_target_pairs={{1,0},{2,1},{3,2},{4,3},{5,4},{6,5},{7,6},{0,7},{9,8},{10,9},{11,1... | collective-permute-start | bytes 492488 | tf_op jit(solution)/shard_map/ppermute | solution.py:19
  37.2 9.7 %collective-permute-start.2 = (f32[10,2,2052]{2,0,1:T(8,128)S(1)}, f32[10,2,2052]{2,0,1:T(8,128)S(1)}, u32[]{:S(2)}, u32[]{:S(2)}) collective-permute-start(f32[10,2,2052]{2,0,1:T(8,128)S(1)} %copy.35), channel_id=1, source_target_pairs={{0,1},{1,2},{2,3},{3,4},{4,5},{5,6},{6,7},{7,0},{8,9},{9,10},{10,1... | collective-permute-start | bytes 492488 | tf_op jit(solution)/shard_map/ppermute | solution.py:17
  39.7 13.6 %copy-start.46 = (f32[16]{0:T(128)}, f32[16]{0:T(128)S(1)}, u32[]{:S(2)}) copy-start(f32[16]{0:T(128)S(1)} %get-tuple-element.42) | copy-start | bytes 196
  39.7 13.6 %copy-start.47 = (f32[16]{0:T(128)}, f32[16]{0:T(128)S(1)}, u32[]{:S(2)}) copy-start(f32[16]{0:T(128)S(1)} %get-tuple-element.43) | copy-start | bytes 196
  40.6 6.4 %copy-start.2 = (f32[10,16,2050]{2,1,0:T(8,128)}, f32[10,16,2050]{2,1,0:T(8,128)S(1)}, u32[]{:S(2)}) copy-start(f32[10,16,2050]{2,1,0:T(8,128)S(1)} %constant_dynamic-update-slice_fusion) | copy-start | bytes 3936004
  47.2 22.8 %copy-start.6 = (s32[32,2,128]{2,0,1:T(8,128)S(1)}, s32[32,2,128]{2,0,1:T(8,128)}, u32[]{:S(2)}) copy-start(s32[32,2,128]{2,0,1:T(8,128)} %fusion.63) | copy-start | bytes 98308
  53.4 17.2 %collective-permute-start.4 = (f32[10,16,2]{2,1,0:T(8,128)S(1)}, f32[10,16,2]{2,1,0:T(8,128)S(1)}, u32[]{:S(2)}, u32[]{:S(2)}) collective-permute-start(f32[10,16,2]{2,1,0:T(8,128)S(1)} %get-tuple-element.15), channel_id=1, source_target_pairs={{0,8},{8,16},{16,24},{24,32},{32,40},{40,48},{48,56},{56,64},{64,7... | collective-permute-start | bytes 3848 | tf_op jit(solution)/shard_map/ppermute | solution.py:17
  55.3 16.2 %collective-permute-start.5 = (f32[10,16,2]{2,1,0:T(8,128)S(1)}, f32[10,16,2]{2,1,0:T(8,128)S(1)}, u32[]{:S(2)}, u32[]{:S(2)}) collective-permute-start(f32[10,16,2]{2,1,0:T(8,128)S(1)} %get-tuple-element.14), channel_id=1, source_target_pairs={{8,0},{16,8},{24,16},{32,24},{40,32},{48,40},{56,48},{64,56},{72,6... | collective-permute-start | bytes 3848 | tf_op jit(solution)/shard_map/ppermute | solution.py:19
  73.0 13.4 %copy-start.8 = (f32[1,2048]{1,0:T(1,128)S(1)}, f32[1,2048]{1,0:T(1,128)}, u32[]{:S(2)}) copy-start(f32[1,2048]{1,0:T(1,128)} %get-tuple-element.27) | copy-start | bytes 24580
  73.0 13.4 %copy-start.10 = (f32[1,2048]{1,0:T(1,128)S(1)}, f32[1,2048]{1,0:T(1,128)}, u32[]{:S(2)}) copy-start(f32[1,2048]{1,0:T(1,128)} %get-tuple-element.28) | copy-start | bytes 24580
  73.0 13.4 %copy-start.12 = (f32[1,2048]{1,0:T(1,128)S(1)}, f32[1,2048]{1,0:T(1,128)}, u32[]{:S(2)}) copy-start(f32[1,2048]{1,0:T(1,128)} %get-tuple-element.29) | copy-start | bytes 24580
  73.0 13.4 %copy-start.14 = (f32[1,2048]{1,0:T(1,128)S(1)}, f32[1,2048]{1,0:T(1,128)}, u32[]{:S(2)}) copy-start(f32[1,2048]{1,0:T(1,128)} %get-tuple-element.30) | copy-start | bytes 24580
  73.0 13.4 %copy-start.16 = (f32[1,2048]{1,0:T(1,128)S(1)}, f32[1,2048]{1,0:T(1,128)}, u32[]{:S(2)}) copy-start(f32[1,2048]{1,0:T(1,128)} %get-tuple-element.31) | copy-start | bytes 24580
  73.0 13.4 %copy-start.18 = (f32[1,2048]{1,0:T(1,128)S(1)}, f32[1,2048]{1,0:T(1,128)}, u32[]{:S(2)}) copy-start(f32[1,2048]{1,0:T(1,128)} %get-tuple-element.32) | copy-start | bytes 24580
  73.0 13.4 %copy-start.20 = (f32[1,2048]{1,0:T(1,128)S(1)}, f32[1,2048]{1,0:T(1,128)}, u32[]{:S(2)}) copy-start(f32[1,2048]{1,0:T(1,128)} %get-tuple-element.33) | copy-start | bytes 24580
  73.0 13.4 %copy-start.22 = (f32[1,2048]{1,0:T(1,128)S(1)}, f32[1,2048]{1,0:T(1,128)}, u32[]{:S(2)}) copy-start(f32[1,2048]{1,0:T(1,128)} %get-tuple-element.34) | copy-start | bytes 24580
  73.0 13.4 %copy-start.24 = (f32[1,2048]{1,0:T(1,128)S(1)}, f32[1,2048]{1,0:T(1,128)}, u32[]{:S(2)}) copy-start(f32[1,2048]{1,0:T(1,128)} %get-tuple-element.35) | copy-start | bytes 24580
  73.0 13.4 %copy-start.26 = (f32[1,2048]{1,0:T(1,128)S(1)}, f32[1,2048]{1,0:T(1,128)}, u32[]{:S(2)}) copy-start(f32[1,2048]{1,0:T(1,128)} %get-tuple-element.36) | copy-start | bytes 24580
  73.0 13.4 %copy-start.28 = (f32[1,2048]{1,0:T(1,128)S(1)}, f32[1,2048]{1,0:T(1,128)}, u32[]{:S(2)}) copy-start(f32[1,2048]{1,0:T(1,128)} %get-tuple-element.37) | copy-start | bytes 24580
  74.6 7.1 %collective-permute-start.7 = (f32[10,2,2052]{2,0,1:T(8,128)S(1)}, f32[10,2,2052]{2,0,1:T(8,128)S(1)}, u32[]{:S(2)}, u32[]{:S(2)}) collective-permute-start(f32[10,2,2052]{2,0,1:T(8,128)S(1)} %copy.41), channel_id=1, source_target_pairs={{1,0},{2,1},{3,2},{4,3},{5,4},{6,5},{7,6},{0,7},{9,8},{10,9},{11,1... | collective-permute-start | bytes 492488 | tf_op jit(solution)/shard_map/ppermute | solution.py:19
  76.6 9.7 %collective-permute-start.6 = (f32[10,2,2052]{2,0,1:T(8,128)S(1)}, f32[10,2,2052]{2,0,1:T(8,128)S(1)}, u32[]{:S(2)}, u32[]{:S(2)}) collective-permute-start(f32[10,2,2052]{2,0,1:T(8,128)S(1)} %copy.39), channel_id=1, source_target_pairs={{0,1},{1,2},{2,3},{3,4},{4,5},{5,6},{6,7},{7,0},{8,9},{9,10},{10,1... | collective-permute-start | bytes 492488 | tf_op jit(solution)/shard_map/ppermute | solution.py:17
  86.4 9.2 %copy-start.36 = (s32[256,1]{0,1:T(1,128)S(1)}, s32[256,1]{0,1:T(1,128)}, u32[]{:S(2)}) copy-start(s32[256,1]{0,1:T(1,128)} %param.15) | copy-start | bytes 3076
  86.5 63.0 %copy-start.39 = (f32[10,10]{1,0:T(8,128)S(1)}, f32[10,10]{1,0:T(8,128)}, u32[]{:S(2)}) copy-start(f32[10,10]{1,0:T(8,128)} %param.14) | copy-start | bytes 1204
  150.5 22.9 %copy-start.40 = (s32[256]{0:T(256)S(1)}, s32[256]{0:T(256)}, u32[]{:S(2)}) copy-start(s32[256]{0:T(256)} %param.17) | copy-start | bytes 3076
  150.5 33.3 %copy-start.48 = (f32[2,10]{1,0:T(2,128)S(1)}, f32[2,10]{1,0:T(2,128)}, u32[]{:S(2)}) copy-start(f32[2,10]{1,0:T(2,128)} %param.19) | copy-start | bytes 244
  150.5 33.5 %copy-start.37 = (f32[2,1,256]{2,1,0:T(1,128)S(1)}, f32[2,1,256]{2,1,0:T(1,128)}, u32[]{:S(2)}) copy-start(f32[2,1,256]{2,1,0:T(1,128)} %get-tuple-element.20) | copy-start | bytes 6148
  150.5 33.5 %copy-start.38 = (f32[2,1,256]{2,1,0:T(1,128)S(1)}, f32[2,1,256]{2,1,0:T(1,128)}, u32[]{:S(2)}) copy-start(f32[2,1,256]{2,1,0:T(1,128)} %get-tuple-element.21) | copy-start | bytes 6148
  163.4 18.6 %all-to-all-start = ((f32[32,1,160]{2,1,0:T(1,128)}), f32[32,1,160]{2,1,0:T(1,128)S(1)}, u32[]{:S(2)}, u32[]{:S(2)}) async-start(f32[32,1,160]{2,1,0:T(1,128)} %reshape.284), calls=%async_computation.1 | async-start | bytes 65536 | tf_op jit(solution)/shard_map/all_to_all | solution.py:96
  184.1 15.7 %copy-start.5 = (f32[2,80,256]{2,1,0:T(8,128)}, f32[2,80,256]{2,1,0:T(8,128)S(1)}, u32[]{:S(2)}) copy-start(f32[2,80,256]{2,1,0:T(8,128)S(1)} %fusion.58) | copy-start | bytes 491524
Sparse Core Ops, SparseCore 0:
  95.8 53.6 reduce-scatter.1
where the time goes:
time: 207 us
  waiting for transfers between devices  75.6 us (37%)
  starting transfers between devices  51.7 us (25%)
  local copies, waits for them, and re-layouts  29.4 us (14%)
  other arithmetic  20.6 us (10%)
  between operations  14.9 us (7%)
  blocking collectives  12.7 us (6%)
    reduce_scatter x1, waiting for transfers between devices, per_device(): lax.psum_scatter(partial_sums, 'lev', scatter_dimension=1, tiled=True)  53.7 us
    ppermute x4, starting transfers between devices, extended_2(): lax.ppermute(head, axis, [((i + 1) % count, i) for i in range(count)])  31.6 us
    all_to_all x1, blocking collectives, per_device(): lax.all_to_all(gathered_exchange_rates, 'patch', split_axis=0, concat_axi...  12.7 us
    scatter x1, local copies, waits for them, and re-layouts, per_device(): outgoing = jnp.zeros((patch_groups, slot_capacity, nflux), jnp.float32).a...  12.1 us
    ppermute x4, starting transfers between devices, extended_2(): lax.ppermute(tail, axis, [(i, (i + 1) % count) for i in range(count)])  10.1 us
    all_to_all x1, starting transfers between devices, per_device(): lax.all_to_all(outgoing, 'patch', split_axis=0, concat_axis=0, tiled=True)  9.93 us
    reduce_sum x1, other arithmetic, per_device(): partial_sums = jnp.sum(q, axis=1)  9.16 us
    ppermute x4, waiting for transfers between devices, extended_2(): lax.ppermute(tail, axis, [(i, (i + 1) % count) for i in range(count)])  8.82 us
  transfers between devices with their start and end apart: 10, of which 7 were waited for; matrix products, arithmetic and copies ran while one was open for 4% of the time, Pallas kernels for 0%

commit v1 on v0

v1 whole, which is shorter than its diff:
```python
import functools
import jax
import jax.numpy as jnp
from jax import lax
from jax.experimental import pallas as pl
from jax.experimental.pallas import tpu as pltpu
from jax.sharding import PartitionSpec as P

F32 = jnp.float32
BF16 = jnp.bfloat16
MESH = pl.DeviceIdType.MESH
DELTAS = (-2, -1, 1, 2)
LANES = 128
HALO = 4


def split_2(x):
    high = x.astype(BF16)
    return high, (x - high.astype(F32)).astype(BF16)


def interval(
    dims,
    atm, offs, edge, rates, mixing, owners, weights, mask, ocean, forcing_mix,
    atm_out, ocean_out, surface_out,
    ring, step1, result, coef, offs_v, edge_v, rates_s, mix_v, owners_v, weights_v, mask_v, ocean_v, base_v, fmix_v,
    edge_send, edge_recv, sums_a, sums_b, got_a, got_b, flux_send, flux_recv, back_send, back_recv, surface_v,
    cols_hot, slot_hot, mix_cols,
    atm_sem, in_sem, edge_sem, lev_send_sem, lev_up_sem, lev_down_sem, sum_sem, flux_sem, back_sem, out_sem,
):
    n_sec, n_patch, n_lev = dims
    ntr, klev, ncol = atm.shape
    alev = klev * n_lev
    block = ncol // n_lev
    slots = weights.shape[0] // n_patch
    copies = LANES // slots
    wide = ncol + 2 * LANES
    rows = klev + 2 * HALO

    sec, patch, lev = lax.axis_index("sec"), lax.axis_index("patch"), lax.axis_index("lev")
    place = sec * n_patch + patch
    n_place = n_sec * n_patch

    def column_neighbour(step):
        other = lax.rem(place + step + n_place, n_place)
        return lax.div(other, n_patch), lax.rem(other, n_patch)

    left, right = column_neighbour(-1), column_neighbour(1)

    def level_of(step):
        return lax.rem(lev + step + n_lev, n_lev)

    small = [
        (offs, offs_v), (edge, edge_v), (rates, rates_s), (owners, owners_v),
        (mixing, mix_v), (forcing_mix, fmix_v), (mask, mask_v), (ocean, ocean_v), (weights, weights_v),
    ]
    loads = [pltpu.make_async_copy(a, b, in_sem.at[i]) for i, (a, b) in enumerate(small)]
    for i in (0, 1):
        loads[i].start()
    atm_loads = [
        pltpu.make_async_copy(atm.at[t], ring.at[t, 0:klev, LANES : LANES + ncol], atm_sem.at[t])
        for t in range(ntr)
    ]
    for load in atm_loads:
        load.start()
    for load in loads[2:]:
        load.start()

    barrier = pltpu.get_barrier_semaphore()

    def greet(where):
        pl.semaphore_signal(barrier, inc=1, device_id=where, device_id_type=MESH)

    for step in (-1, 0, 1):
        for s, p in (left, right):
            greet((s, p, level_of(step)))
    for i in range(1, n_lev):
        greet((sec, patch, level_of(i)))

    def greet_patch(i, carry):
        greet((sec, lax.rem(patch + i, n_patch), lev))
        return carry

    lax.fori_loop(1, n_patch, greet_patch, 0)

    loads[0].wait()
    loads[1].wait()
    offsets, exchange = offs_v[...], edge_v[...]
    total = jnp.zeros((1, ncol), F32)
    for i, delta in enumerate(DELTAS):
        part = jnp.sum(jnp.where(offsets == delta, exchange, 0.0), axis=0, keepdims=True)
        total = total + part
        coef[i, :, LANES : LANES + ncol] = jnp.broadcast_to(part, (8, ncol))
    coef[4, :, LANES : LANES + ncol] = jnp.broadcast_to(1.0 - total, (8, ncol))

    lane = lax.broadcasted_iota(jnp.int32, (8, LANES), 1)
    row = lax.broadcasted_iota(jnp.int32, (8, LANES), 0)
    coef_lane = 2 * ntr * HALO
    for load in atm_loads:
        load.wait()
    first = jnp.zeros((8, LANES), F32)
    last = jnp.zeros((8, LANES), F32)
    for t in range(ntr):
        for k in range(2):
            at = (2 * t + k) * HALO
            here = (lane >= at) & (lane < at + HALO)
            a = ring[t, 8 * k : 8 * k + 8, LANES : 2 * LANES]
            b = ring[t, 8 * k : 8 * k + 8, ncol : ncol + LANES]
            first = jnp.where(here, pltpu.roll(a, at, 1) if at else a, first)
            last = jnp.where(here, pltpu.roll(b, at + HALO, 1), last)
    here = (lane >= coef_lane) & (lane < coef_lane + HALO)
    for i in range(4):
        a = coef[i, :, LANES : 2 * LANES]
        b = coef[i, :, ncol : ncol + LANES]
        first = jnp.where(here & (row == i), pltpu.roll(a, coef_lane, 1), first)
        last = jnp.where(here & (row == i), pltpu.roll(b, coef_lane + HALO, 1), last)
    edge_send[0] = first
    edge_send[1] = last

    pl.semaphore_wait(barrier, 6 + (n_lev - 1) + (n_patch - 1))

    for side, (s, p) in ((0, right), (1, left)):
        for step in (0, -1, 1):
            pltpu.make_async_remote_copy(
                src_ref=edge_send.at[1 - side],
                dst_ref=edge_recv.at[side, 1 - step],
                send_sem=edge_sem.at[0],
                recv_sem=edge_sem.at[1],
                device_id=(s, p, level_of(step)),
                device_id_type=MESH,
            ).start()

    def to_lower(t):
        return pltpu.make_async_remote_copy(
            src_ref=atm.at[t, 0:HALO, :],
            dst_ref=ring.at[t, klev : klev + HALO, LANES : LANES + ncol],
            send_sem=lev_send_sem.at[0, t],
            recv_sem=lev_up_sem.at[t],
            device_id=(sec, patch, level_of(-1)),
            device_id_type=MESH,
        )

    def to_upper(t):
        return pltpu.make_async_remote_copy(
            src_ref=atm.at[t, klev - HALO : klev, :],
            dst_ref=ring.at[t, klev + HALO : rows, LANES : LANES + ncol],
            send_sem=lev_send_sem.at[1, t],
            recv_sem=lev_down_sem.at[t],
            device_id=(sec, patch, level_of(1)),
            device_id_type=MESH,
        )

    @pl.when(lev > 0)
    def _():
        for t in range(ntr):
            to_lower(t).start()

    @pl.when(lev < n_lev - 1)
    def _():
        for t in range(ntr):
            to_upper(t).start()

    @pl.when(lev == 0)
    def _():
        ring[:, klev + HALO : rows, LANES : LANES + ncol] = jnp.zeros((ntr, HALO, ncol), F32)

    @pl.when(lev == n_lev - 1)
    def _():
        ring[:, klev : klev + HALO, LANES : LANES + ncol] = jnp.zeros((ntr, HALO, ncol), F32)

    for load in loads[2:]:
        load.wait()
    owned = owners_v[...]
    hot = (lax.broadcasted_iota(jnp.int32, (n_patch, block), 0) == owned).astype(F32)
    cols_hot[...] = hot
    earlier = (
        lax.broadcasted_iota(jnp.int32, (block, block), 0) < lax.broadcasted_iota(jnp.int32, (block, block), 1)
    ).astype(F32).astype(BF16)
    rank = jnp.dot(hot.astype(BF16), earlier, preferred_element_type=F32)
    slot = jnp.sum(rank * hot, axis=0, keepdims=True).astype(jnp.int32)
    lane_slot = lax.rem(lax.broadcasted_iota(jnp.int32, (LANES, block), 0), slots)
    slot_hot[...] = (lane_slot == slot).astype(F32).astype(BF16)
    for t in range(ntr):
        mix_cols[t] = jnp.broadcast_to(mix_v[:, t : t + 1], (mixing.shape[0], block))

    state = ocean_v[...]
    nol = state.shape[1]
    level = lax.broadcasted_iota(jnp.int32, state.shape, 1)
    above = jnp.where(level < nol - 1, pltpu.roll(state, nol - 1, 1) - state, 0.0)
    below = jnp.where(level > 0, pltpu.roll(state, 1, 1) - state, 0.0)
    base_v[...] = state + 0.2 * above + 0.2 * below

    pltpu.make_async_copy(edge_recv, edge_recv, edge_sem.at[1]).wait()
    beside = jnp.where(
        lane < LANES // 2,
        pltpu.roll(edge_recv[1, 1], LANES - coef_lane, 1),
        pltpu.roll(edge_recv[0, 1], LANES - HALO - coef_lane, 1),
    )
    total = jnp.zeros((1, LANES), F32)
    for i in range(4):
        part = beside[i : i + 1, :]
        total = total + part
        for at in (0, LANES + ncol):
            coef[i, :, at : at + LANES] = jnp.broadcast_to(part, (8, LANES))
    for at in (0, LANES + ncol):
        coef[4, :, at : at + LANES] = jnp.broadcast_to(1.0 - total, (8, LANES))

    ring_row = lax.broadcasted_iota(jnp.int32, (rows, LANES), 0)
    k = lev * klev + jnp.where(ring_row < klev + HALO, ring_row, ring_row - rows)
    inside = (k >= 0) & (k < alev)
    vertical = (
        3.0
        - (k < 1).astype(F32) - 0.5 * (k < 2).astype(F32)
        - (k > alev - 2).astype(F32) - 0.5 * (k > alev - 3).astype(F32)
    )
    inside_halo = inside[klev:, :]

    def across(x, times):
        return jnp.concatenate([x] * times, axis=1) if times > 1 else x

    def down(x):
        return jnp.concatenate([x] * (rows // 8), axis=0)

    def stencil(x, at, tiles, rate, rate_vertical):
        width = tiles * LANES
        middle = x[:, LANES : LANES + width]
        out = middle * (down(coef[4, :, at : at + width]) - across(rate_vertical, tiles))
        for i, delta in enumerate(DELTAS):
            moved = pltpu.roll(x, (-delta) % x.shape[1], 1)[:, LANES : LANES + width]
            out = out + down(coef[i, :, at : at + width]) * moved
        one = pltpu.roll(middle, 1, 0) + pltpu.roll(middle, rows - 1, 0)
        two = pltpu.roll(middle, 2, 0) + pltpu.roll(middle, rows - 2, 0)
        return out + rate * (one + 0.5 * two)

    def masked(x, tiles):
        return jnp.concatenate(
            [x[:klev], jnp.where(across(inside_halo, tiles), x[klev:], 0.0)], axis=0
        )

    tiles = 4
    chunk = tiles * LANES

    def tracer(t, sums, at_row):
        @pl.when(lev < n_lev - 1)
        def _():
            to_lower(t).wait_recv()

        @pl.when(lev > 0)
        def _():
            to_upper(t).wait_recv()

        rate = rates_s[t]
        rate_vertical = rate * vertical
        low, high = 2 * HALO * t, 2 * HALO * t + HALO

        def sides(from_left, from_right, lanes_at):
            return jnp.where(
                lane < LANES // 2,
                pltpu.roll(from_right, lax.rem(LANES - lanes_at, LANES), 1),
                pltpu.roll(from_left, LANES - HALO - lanes_at, 1),
            )

        corner = jnp.where(
            row < HALO,
            sides(edge_recv[0, 2], edge_recv[1, 2], low),
            sides(edge_recv[0, 0], edge_recv[1, 0], high),
        )
        halo = jnp.concatenate(
            [
                sides(edge_recv[0, 1], edge_recv[1, 1], low),
                sides(edge_recv[0, 1], edge_recv[1, 1], high),
                jnp.where(inside_halo, corner, 0.0),
            ],
            axis=0,
        )
        ring[t, :, 0:LANES] = halo
        ring[t, :, LANES + ncol : wide] = halo

        x = jnp.concatenate([ring[t, :, ncol : ncol + LANES], halo, ring[t, :, LANES : 2 * LANES]], axis=1)
        halo = masked(stencil(x, 0, 1, rate, rate_vertical), 1)
        step1[:, 0:LANES] = halo
        step1[:, LANES + ncol : wide] = halo
        for c in range(ncol // chunk):
            at = LANES + c * chunk
            x = ring[t, :, at - LANES : at + chunk + LANES]
            step1[:, at : at + chunk] = masked(stencil(x, at, tiles, rate, rate_vertical), tiles)
        for c in range(ncol // chunk):
            at = LANES + c * chunk
            x = step1[:, at - LANES : at + chunk + LANES]
            out = stencil(x, at, tiles, rate, rate_vertical)[:klev]
            result[t, :, c * chunk : (c + 1) * chunk] = out
            column_sums = jnp.sum(out, axis=0, keepdims=True)
            for i in range(chunk // block):
                sums[c * (chunk // block) + i, pl.ds(at_row, 1), :] = column_sums[:, i * block : (i + 1) * block]
        pltpu.make_async_copy(result.at[t], atm_out.at[t], out_sem.at[0]).start()

    n_a = sums_a.shape[1]

    def send_sums(sums, got, which):
        for i in range(1, n_lev):
            pltpu.make_async_remote_copy(
                src_ref=sums.at[level_of(i)],
                dst_ref=got.at[n_lev - 1 - i],
                send_sem=sum_sem.at[0, which],
                recv_sem=sum_sem.at[1, which],
                device_id=(sec, patch, level_of(i)),
                device_id_type=MESH,
            ).start()

    def tracer_a(t, carry):
        tracer(t, sums_a, t)
        return carry

    def tracer_b(t, carry):
        tracer(t, sums_b, t - n_a)
        return carry

    lax.fori_loop(0, n_a, tracer_a, 0)
    send_sums(sums_a, got_a, 0)
    lax.fori_loop(n_a, ntr, tracer_b, 0)
    send_sums(sums_b, got_b, 1)

    pick = (
        lax.broadcasted_iota(jnp.int32, (ntr, ntr), 0) == lax.broadcasted_iota(jnp.int32, (ntr, ntr), 1)
    )
    fmix = fmix_v[...]
    fmix_cols = [
        jnp.sum(jnp.where(pick, jnp.broadcast_to(fmix[v : v + 1, :], (ntr, ntr)), 0.0), axis=1, keepdims=True)
        for v in range(2)
    ]

    def level_sums(sums, got, which):
        pltpu.make_async_copy(got, got, sum_sem.at[1, which]).wait()
        out = sums[lev]
        for i in range(n_lev - 1):
            out = out + got[i]
        return out

    mean_a = level_sums(sums_a, got_a, 0) * (1.0 / alev)
    mixed = jnp.zeros((mixing.shape[0], block), F32)
    for t in range(n_a):
        mixed = mixed + mix_cols[t] * mean_a[t : t + 1, :]
    mean_b = level_sums(sums_b, got_b, 1) * (1.0 / alev)
    for t in range(n_a, ntr):
        mixed = mixed + mix_cols[t] * mean_b[t - n_a : t - n_a + 1, :]
    flux = jnp.tanh(mixed)
    hot = cols_hot[...]
    parts = []
    for v in range(2):
        forced = jnp.sum(fmix_cols[v] * flux, axis=0, keepdims=True)
        parts += [(hot * piece.astype(F32)).astype(BF16) for piece in split_2(forced)]
    slot_map = slot_hot[...]
    out = lax.dot_general(
        jnp.concatenate(parts, axis=0), slot_map, (((1,), (1,)), ((), ())), preferred_element_type=F32
    )
    outgoing = [out[2 * v * n_patch : (2 * v + 1) * n_patch] + out[(2 * v + 1) * n_patch : (2 * v + 2) * n_patch] for v in range(2)]
    for v in range(2):
        flux_send[:, v * LANES : (v + 1) * LANES] = outgoing[v]

    def send_flux(i, carry):
        other = lax.rem(patch + i, n_patch)
        pltpu.make_async_remote_copy(
            src_ref=flux_send.at[pl.ds(other, 1), :],
            dst_ref=flux_recv.at[pl.ds(patch, 1), :],
            send_sem=flux_sem.at[0],
            recv_sem=flux_sem.at[1],
            device_id=(sec, other, lev),
            device_id_type=MESH,
        ).start()
        return carry

    lax.fori_loop(1, n_patch, send_flux, 0)
    own_row = pl.ds(patch, 1)
    pltpu.make_async_copy(flux_send.at[own_row, :], flux_recv.at[own_row, :], flux_sem.at[1]).start()
    ocean_cells = mask_v[...].astype(F32)
    pltpu.make_async_copy(flux_recv, flux_recv, flux_sem.at[1]).wait()

    groups = n_patch * slots // LANES
    received = []
    for v in range(2):
        pieces = []
        for g in range(groups):
            tile = flux_recv[g * copies : (g + 1) * copies, v * LANES : (v + 1) * LANES]
            pieces.append(jnp.sum(jnp.where(lax.div(lane, slots) == row, tile, 0.0), axis=0, keepdims=True))
        received.append(jnp.concatenate(pieces, axis=1))
    w = weights_v[...]

    def stacked(values):
        at = lax.broadcasted_iota(jnp.int32, (16, values[0].shape[1]), 0)
        out = jnp.zeros((16, values[0].shape[1]), F32)
        for i, value in enumerate(values):
            out = jnp.where(at == i, value.astype(F32), out)
        return out.astype(BF16)

    sums = jnp.dot(stacked([*split_2(received[0]), *split_2(received[1])]), w, preferred_element_type=F32)
    forcing = [(sums[2 * v : 2 * v + 1] + sums[2 * v + 1 : 2 * v + 2]) * ocean_cells for v in range(2)]
    warmth = (base_v[0, 0:1, :] + forcing[0]) * ocean_cells
    back = lax.dot_general(
        stacked([*split_2(warmth)]), w, (((1,), (1,)), ((), ())), preferred_element_type=F32
    )
    back = back[0:1] + back[1:2]
    for g in range(groups):
        back_send[g : g + 1, :] = back[:, g * LANES : (g + 1) * LANES]

    def send_back(i, carry):
        other = lax.rem(patch + i, n_patch)
        pltpu.make_async_remote_copy(
            src_ref=back_send.at[pl.ds(lax.div(other, copies), 1), :],
            dst_ref=back_recv.at[pl.ds(patch, 1), :],
            send_sem=back_sem.at[0],
            recv_sem=back_sem.at[1],
            device_id=(sec, other, lev),
            device_id_type=MESH,
        ).start()
        return carry

    lax.fori_loop(1, n_patch, send_back, 0)
    pltpu.make_async_copy(
        back_send.at[pl.ds(lax.div(patch, copies), 1), :], back_recv.at[own_row, :], back_sem.at[1]
    ).start()

    depth = lax.broadcasted_iota(jnp.int32, (nol, block), 0).astype(F32)
    profile = jnp.exp(-depth / 8.0)
    for v in range(2):
        ocean_v[v] = base_v[v] + profile * forcing[v]
    pltpu.make_async_copy(ocean_v, ocean_out, out_sem.at[1]).start()

    pltpu.make_async_copy(back_recv, back_recv, back_sem.at[1]).wait()
    at_lane = lax.broadcasted_iota(jnp.int32, (n_patch, LANES), 1)
    own = lax.div(at_lane, slots) == lax.rem(patch, copies)
    returned = jnp.where(own, back_recv[...], 0.0)
    values = jnp.dot(jnp.concatenate(split_2(returned), axis=0), slot_map, preferred_element_type=F32)
    surface_v[...] = jnp.sum((values[:n_patch] + values[n_patch:]) * hot, axis=0, keepdims=True)
    pltpu.make_async_copy(surface_v, surface_out, out_sem.at[2]).start()

    six = edge_recv
    pltpu.make_async_copy(six, six, edge_sem.at[0]).wait()

    @pl.when(lev > 0)
    def _():
        for t in range(ntr):
            to_lower(t).wait_send()

    @pl.when(lev < n_lev - 1)
    def _():
        for t in range(ntr):
            to_upper(t).wait_send()

    pltpu.make_async_copy(got_a, got_a, sum_sem.at[0, 0]).wait()
    pltpu.make_async_copy(got_b, got_b, sum_sem.at[0, 1]).wait()
    count = n_patch // 2
    while count:
        for ref, sem in ((flux_recv, flux_sem), (back_recv, back_sem)):
            some = ref.at[pl.ds(0, count), :]
            pltpu.make_async_copy(some, some, sem.at[0]).wait()
        count //= 2
    pltpu.make_async_copy(result, atm_out, out_sem.at[0]).wait()
    pltpu.make_async_copy(ocean_v, ocean_out, out_sem.at[1]).wait()
    pltpu.make_async_copy(surface_v, surface_out, out_sem.at[2]).wait()


def solution(mesh):
    dims = tuple(mesh.shape[a] for a in ("sec", "patch", "lev"))
    n_sec, n_patch, n_lev = dims

    def per_device(atm, offs, edge, rates, mixing, owners, weights, mask, ocean, forcing_mix):
        ntr, klev, ncol = atm.shape
        rows, wide = klev + 2 * HALO, ncol + 2 * LANES
        block = ncol // n_lev
        nflux = mixing.shape[0]
        owners, mask = owners.reshape(1, -1), mask.reshape(1, -1)
        dma = pltpu.SemaphoreType.DMA
        vmem = pltpu.VMEM
        any_space = pl.BlockSpec(memory_space=pl.ANY)
        out = pl.pallas_call(
            functools.partial(interval, dims),
            out_shape=(
                jax.ShapeDtypeStruct(atm.shape, F32),
                jax.ShapeDtypeStruct(ocean.shape, F32),
                jax.ShapeDtypeStruct((1, block), F32),
            ),
            in_specs=[any_space] * 10,
            out_specs=(any_space,) * 3,
            scratch_shapes=[
                vmem((ntr, rows, wide), F32),
                vmem((rows, wide), F32),
                vmem(atm.shape, F32),
                vmem((5, 8, wide), F32),
                vmem(offs.shape, jnp.int32),
                vmem(edge.shape, F32),
                pltpu.SMEM(rates.shape, F32),
                vmem(mixing.shape, F32),
                vmem(owners.shape, jnp.int32),
                vmem(weights.shape, BF16),
                vmem(mask.shape, jnp.int32),
                vmem(ocean.shape, F32),
                vmem(ocean.shape, F32),
                vmem(forcing_mix.shape, F32),
                vmem((2, 8, LANES), F32),
                vmem((2, 3, 8, LANES), F32),
                vmem((n_lev, 8, block), F32),
                vmem((n_lev, ntr - 8, block), F32),
                vmem((n_lev - 1, 8, block), F32),
                vmem((n_lev - 1, ntr - 8, block), F32),
                vmem((n_patch, 2 * LANES), F32),
                vmem((n_patch, 2 * LANES), F32),
                vmem((weights.shape[0] // LANES, LANES), F32),
                vmem((n_patch, LANES), F32),
                vmem((1, block), F32),
                vmem((n_patch, block), F32),
                vmem((LANES, block), BF16),
                vmem((ntr, nflux, block), F32),
                dma((ntr,)),
                dma((9,)),
                dma((2,)),
                dma((2, ntr)),
                dma((ntr,)),
                dma((ntr,)),
                dma((2, 2)),
                dma((2,)),
                dma((2,)),
                dma((3,)),
            ],
            compiler_params=pltpu.CompilerParams(
                collective_id=0, has_side_effects=True, vmem_limit_bytes=32 * 1024 * 1024
            ),
            name="interval",
        )(atm, offs, edge, rates, mixing, owners, weights, mask, ocean, forcing_mix)
        return out[0], out[1], out[2].reshape(-1)

    in_specs = (
        P(None, "lev", ("sec", "patch")),
        P(None, ("sec", "patch")),
        P(None, ("sec", "patch")),
        P(),
        P(),
        P(("sec", "patch", "lev"), None),
        P(None, ("sec", "patch", "lev")),
        P(("sec", "patch", "lev")),
        P(None, None, ("sec", "patch", "lev")),
        P(),
    )
    out_specs = (
        P(None, "lev", ("sec", "patch")),
        P(None, None, ("sec", "patch", "lev")),
        P(("sec", "patch", "lev")),
    )
    return jax.shard_map(per_device, mesh=mesh, in_specs=in_specs, out_specs=out_specs, check_vma=False)
```

time: 207 us -> 65.2 us (0.31)
  the two profiles are of different devices: /device:TPU:2 before, /device:TPU:1 now
where the time goes in v1:
time: 65.2 us; the launch traced here: 64.8 us
  Pallas kernels  53.7 us (82%)
  local copies, waits for them, and re-layouts  10.4 us (16%)
  between operations  0.66 us (1%)
    pallas_call x1, Pallas kernels, per_device(): pl.pallas_call(functools.partial(interval, dims), out_shape=(jax.ShapeDty...  53.7 us
    unnamed x23, local copies, waits for them, and re-layouts  10.4 us

profile of v1, /device:TPU:1, one launch (start us, length us, event | category | flops | bytes accessed | tf_op | source)
XLA Modules:
  0.0 64.8 jit_solution(6275834265462916629)
XLA Ops:
  0.6 0.0 copy-start
  0.6 1.3 %copy-done = f32[10,16,2048]{2,1,0:T(8,128)S(1)} copy-done((f32[10,16,2048]{2,1,0:T(8,128)S(1)}, f32[10,16,2048]{2,1,0:T(8,128)}, u32[]{:S(2)}) %copy-start) | copy-done | bytes 1310744
  2.0 0.0 copy-start.1
  2.0 0.9 %copy-done.1 = bf16[512,256]{1,0:T(8,128)(2,1)S(1)} copy-done((bf16[512,256]{1,0:T(8,128)(2,1)S(1)}, bf16[512,256]{1,0:T(8,128)(2,1)}, u32[]{:S(2)}) %copy-start.1) | copy-done | bytes 262168
  2.9 0.0 copy-start.2
  2.9 0.9 %copy-done.2 = f32[2,80,256]{2,1,0:T(8,128)S(1)} copy-done((f32[2,80,256]{2,1,0:T(8,128)S(1)}, f32[2,80,256]{2,1,0:T(8,128)}, u32[]{:S(2)}) %copy-start.2) | copy-done | bytes 163864
  3.8 0.0 copy-start.3
  3.8 0.8 %copy-done.3 = s32[3,2048]{1,0:T(4,128)S(1)} copy-done((s32[3,2048]{1,0:T(4,128)S(1)}, s32[3,2048]{1,0:T(4,128)}, u32[]{:S(2)}) %copy-start.3) | copy-done | bytes 24600
  4.6 0.0 copy-start.4
  4.6 0.8 %copy-done.4 = f32[3,2048]{1,0:T(4,128)S(1)} copy-done((f32[3,2048]{1,0:T(4,128)S(1)}, f32[3,2048]{1,0:T(4,128)}, u32[]{:S(2)}) %copy-start.4) | copy-done | bytes 24600
  5.3 0.0 copy-start.5
  5.3 0.7 %copy-done.5 = f32[10,10]{1,0:T(8,128)S(1)} copy-done((f32[10,10]{1,0:T(8,128)S(1)}, f32[10,10]{1,0:T(8,128)}, u32[]{:S(2)}) %copy-start.5) | copy-done | bytes 424
  6.0 0.0 copy-start.6
  6.0 0.7 %copy-done.6 = s32[256,1]{0,1:T(1,128)S(1)} copy-done((s32[256,1]{0,1:T(1,128)S(1)}, s32[256,1]{0,1:T(1,128)}, u32[]{:S(2)}) %copy-start.6) | copy-done | bytes 1048
  6.7 0.0 copy-start.7
  6.7 0.7 %copy-done.7 = s32[256]{0:T(256)S(1)} copy-done((s32[256]{0:T(256)S(1)}, s32[256]{0:T(256)}, u32[]{:S(2)}) %copy-start.7) | copy-done | bytes 1048
  7.4 0.0 copy-start.8
  7.4 0.7 %copy-done.8 = f32[2,10]{1,0:T(2,128)S(1)} copy-done((f32[2,10]{1,0:T(2,128)S(1)}, f32[2,10]{1,0:T(2,128)}, u32[]{:S(2)}) %copy-start.8) | copy-done | bytes 104
  8.1 0.0 copy-start.9
  8.1 0.7 %copy-done.9 = f32[10]{0:T(128)S(1)} copy-done((f32[10]{0:T(128)S(1)}, f32[10]{0:T(128)}, u32[]{:S(2)}) %copy-start.9) | copy-done | bytes 64
  8.7 53.7 %interval.1 = (f32[10,16,2048]{2,1,0:T(8,128)S(1)}, f32[2,80,256]{2,1,0:T(8,128)S(1)}, f32[1,256]{1,0:T(1,128)S(1)}) custom-call(f32[10,16,2048]{2,1,0:T(8,128)S(1)} %copy-done, s32[3,2048]{1,0:T(4,128)S(1)} %copy-done.3, f32[3,2048]{1,0:T(4,128)S(1)} %copy-done.4, f32[10]{0:T(128)S(1)} %copy-done.9, f32[10,10]{1,0:T(8,128)S(1)} %copy-done.5, ...), custom_call_target="tpu_custom_call" | custom-call | tf_op jit(solution)/shard_map/interval/pallas_call | solution.py:475
  62.5 1.1 %copy.16 = f32[10,16,2048]{2,1,0:T(8,128)} copy(f32[10,16,2048]{2,1,0:T(8,128)S(1)} %get-tuple-element.12) | data formatting | bytes 2621440
  63.5 0.7 %copy.17 = f32[2,80,256]{2,1,0:T(8,128)} copy(f32[2,80,256]{2,1,0:T(8,128)S(1)} %get-tuple-element.13) | data formatting | bytes 327680
  64.2 0.6 copy.18
Async XLA Ops:
  0.6 1.3 %copy-start = (f32[10,16,2048]{2,1,0:T(8,128)S(1)}, f32[10,16,2048]{2,1,0:T(8,128)}, u32[]{:S(2)}) copy-start(f32[10,16,2048]{2,1,0:T(8,128)} %atm.1) | copy-start | bytes 3932164
  2.0 0.9 %copy-start.1 = (bf16[512,256]{1,0:T(8,128)(2,1)S(1)}, bf16[512,256]{1,0:T(8,128)(2,1)}, u32[]{:S(2)}) copy-start(bf16[512,256]{1,0:T(8,128)(2,1)} %weights.1) | copy-start | bytes 786436
  2.9 0.9 %copy-start.2 = (f32[2,80,256]{2,1,0:T(8,128)S(1)}, f32[2,80,256]{2,1,0:T(8,128)}, u32[]{:S(2)}) copy-start(f32[2,80,256]{2,1,0:T(8,128)} %ocean.1) | copy-start | bytes 491524
  3.8 0.8 %copy-start.3 = (s32[3,2048]{1,0:T(4,128)S(1)}, s32[3,2048]{1,0:T(4,128)}, u32[]{:S(2)}) copy-start(s32[3,2048]{1,0:T(4,128)} %offs.1) | copy-start | bytes 73732
  4.6 0.8 %copy-start.4 = (f32[3,2048]{1,0:T(4,128)S(1)}, f32[3,2048]{1,0:T(4,128)}, u32[]{:S(2)}) copy-start(f32[3,2048]{1,0:T(4,128)} %edge.1) | copy-start | bytes 73732
  5.3 0.7 %copy-start.5 = (f32[10,10]{1,0:T(8,128)S(1)}, f32[10,10]{1,0:T(8,128)}, u32[]{:S(2)}) copy-start(f32[10,10]{1,0:T(8,128)} %mixing.1) | copy-start | bytes 1204
  6.0 0.7 %copy-start.6 = (s32[256,1]{0,1:T(1,128)S(1)}, s32[256,1]{0,1:T(1,128)}, u32[]{:S(2)}) copy-start(s32[256,1]{0,1:T(1,128)} %param.15) | copy-start | bytes 3076
  6.7 0.7 %copy-start.7 = (s32[256]{0:T(256)S(1)}, s32[256]{0:T(256)}, u32[]{:S(2)}) copy-start(s32[256]{0:T(256)} %param.17) | copy-start | bytes 3076
  7.4 0.7 %copy-start.8 = (f32[2,10]{1,0:T(2,128)S(1)}, f32[2,10]{1,0:T(2,128)}, u32[]{:S(2)}) copy-start(f32[2,10]{1,0:T(2,128)} %forcing_mix.1) | copy-start | bytes 244
  8.1 0.7 %copy-start.9 = (f32[10]{0:T(128)S(1)}, f32[10]{0:T(128)}, u32[]{:S(2)}) copy-start(f32[10]{0:T(128)} %rates.1) | copy-start | bytes 124

commit v2 on v1

--- a/solution.py
+++ b/solution.py
@@ -22,11 +22,11 @@
 def interval(
     dims,
     atm, offs, edge, rates, mixing, owners, weights, mask, ocean, forcing_mix,
-    atm_out, ocean_out, surface_out,
-    ring, step1, result, coef, offs_v, edge_v, rates_s, mix_v, owners_v, weights_v, mask_v, ocean_v, base_v, fmix_v,
-    edge_send, edge_recv, sums_a, sums_b, got_a, got_b, flux_send, flux_recv, back_send, back_recv, surface_v,
+    result, ocean_new, surface_new,
+    ring, step1, coef, offs_v, edge_v, rates_s, mix_v, owners_v, weights_v, mask_v, ocean_v, base_v, fmix_v,
+    edge_send, edge_recv, sums_a, sums_b, got_a, got_b, flux_send, flux_recv, back_send, back_recv,
     cols_hot, slot_hot, mix_cols,
-    atm_sem, in_sem, edge_sem, lev_send_sem, lev_up_sem, lev_down_sem, sum_sem, flux_sem, back_sem, out_sem,
+    atm_sem, in_sem, edge_sem, lev_send_sem, lev_up_sem, lev_down_sem, sum_sem, flux_sem, back_sem,
 ):
     n_sec, n_patch, n_lev = dims
     ntr, klev, ncol = atm.shape
@@ -49,6 +49,23 @@
 
     def level_of(step):
         return lax.rem(lev + step + n_lev, n_lev)
+
+    barrier = pltpu.get_barrier_semaphore()
+
+    def greet(where):
+        pl.semaphore_signal(barrier, inc=1, device_id=where, device_id_type=MESH)
+
+    for step in (-1, 0, 1):
+        for s, p in (left, right):
+            greet((s, p, level_of(step)))
+    for i in range(1, n_lev):
+        greet((sec, patch, level_of(i)))
+
+    def greet_patch(i, carry):
+        greet((sec, lax.rem(patch + i, n_patch), lev))
+        return carry
+
+    lax.fori_loop(1, n_patch, greet_patch, 0)
 
     small = [
         (offs, offs_v), (edge, edge_v), (rates, rates_s), (owners, owners_v),
@@ -65,23 +82,6 @@
         load.start()
     for load in loads[2:]:
         load.start()
-
-    barrier = pltpu.get_barrier_semaphore()
-
-    def greet(where):
-        pl.semaphore_signal(barrier, inc=1, device_id=where, device_id_type=MESH)
-
-    for step in (-1, 0, 1):
-        for s, p in (left, right):
-            greet((s, p, level_of(step)))
-    for i in range(1, n_lev):
-        greet((sec, patch, level_of(i)))
-
-    def greet_patch(i, carry):
-        greet((sec, lax.rem(patch + i, n_patch), lev))
-        return carry
-
-    lax.fori_loop(1, n_patch, greet_patch, 0)
 
     loads[0].wait()
     loads[1].wait()
@@ -190,21 +190,6 @@
     below = jnp.where(level > 0, pltpu.roll(state, 1, 1) - state, 0.0)
     base_v[...] = state + 0.2 * above + 0.2 * below
 
-    pltpu.make_async_copy(edge_recv, edge_recv, edge_sem.at[1]).wait()
-    beside = jnp.where(
-        lane < LANES // 2,
-        pltpu.roll(edge_recv[1, 1], LANES - coef_lane, 1),
-        pltpu.roll(edge_recv[0, 1], LANES - HALO - coef_lane, 1),
-    )
-    total = jnp.zeros((1, LANES), F32)
-    for i in range(4):
-        part = beside[i : i + 1, :]
-        total = total + part
-        for at in (0, LANES + ncol):
-            coef[i, :, at : at + LANES] = jnp.broadcast_to(part, (8, LANES))
-    for at in (0, LANES + ncol):
-        coef[4, :, at : at + LANES] = jnp.broadcast_to(1.0 - total, (8, LANES))
-
     ring_row = lax.broadcasted_iota(jnp.int32, (rows, LANES), 0)
     k = lev * klev + jnp.where(ring_row < klev + HALO, ring_row, ring_row - rows)
     inside = (k >= 0) & (k < alev)
@@ -237,10 +222,26 @@
             [x[:klev], jnp.where(across(inside_halo, tiles), x[klev:], 0.0)], axis=0
         )
 
-    tiles = 4
-    chunk = tiles * LANES
-
-    def tracer(t, sums, at_row):
+    n_tiles = ncol // LANES
+    per_block = block // LANES
+    n_a = sums_a.shape[2]
+
+    def step_1(t, first, tiles, rate, rate_vertical):
+        at = LANES * (1 + first)
+        x = ring[t, :, at - LANES : at + (tiles + 1) * LANES]
+        step1[t, :, at : at + tiles * LANES] = masked(stencil(x, at, tiles, rate, rate_vertical), tiles)
+
+    def step_2(t, first, tiles, rate, rate_vertical, sums, at_row):
+        at = LANES * (1 + first)
+        x = step1[t, :, at - LANES : at + (tiles + 1) * LANES]
+        out = stencil(x, at, tiles, rate, rate_vertical)[:klev]
+        result[t, :, at - LANES : at + (tiles - 1) * LANES] = out
+        column_sums = jnp.sum(out, axis=0, keepdims=True)
+        for i in range(tiles):
+            d, half = divmod(first + i, per_block)
+            sums[d, half, pl.ds(at_row, 1), :] = column_sums[:, i * LANES : (i + 1) * LANES]
+
+    def inner(t, sums, at_row):
         @pl.when(lev < n_lev - 1)
         def _():
             to_lower(t).wait_recv()
@@ -249,6 +250,15 @@
         def _():
             to_upper(t).wait_recv()
 
+        rate = rates_s[t]
+        rate_vertical = rate * vertical
+        for first in range(0, n_tiles, 4):
+            step_1(t, first, 4, rate, rate_vertical)
+        for first in range(0, n_tiles, 4):
+            low, high = max(first, 1), min(first + 4, n_tiles - 1)
+            step_2(t, low, high - low, rate, rate_vertical, sums, at_row)
+
+    def outer(t, sums, at_row):
         rate = rates_s[t]
         rate_vertical = rate * vertical
         low, high = 2 * HALO * t, 2 * HALO * t + HALO
@@ -278,47 +288,59 @@
 
         x = jnp.concatenate([ring[t, :, ncol : ncol + LANES], halo, ring[t, :, LANES : 2 * LANES]], axis=1)
         halo = masked(stencil(x, 0, 1, rate, rate_vertical), 1)
-        step1[:, 0:LANES] = halo
-        step1[:, LANES + ncol : wide] = halo
-        for c in range(ncol // chunk):
-            at = LANES + c * chunk
-            x = ring[t, :, at - LANES : at + chunk + LANES]
-            step1[:, at : at + chunk] = masked(stencil(x, at, tiles, rate, rate_vertical), tiles)
-        for c in range(ncol // chunk):
-            at = LANES + c * chunk
-            x = step1[:, at - LANES : at + chunk + LANES]
-            out = stencil(x, at, tiles, rate, rate_vertical)[:klev]
-            result[t, :, c * chunk : (c + 1) * chunk] = out
-            column_sums = jnp.sum(out, axis=0, keepdims=True)
-            for i in range(chunk // block):
-                sums[c * (chunk // block) + i, pl.ds(at_row, 1), :] = column_sums[:, i * block : (i + 1) * block]
-        pltpu.make_async_copy(result.at[t], atm_out.at[t], out_sem.at[0]).start()
-
-    n_a = sums_a.shape[1]
-
-    def send_sums(sums, got, which):
-        for i in range(1, n_lev):
-            pltpu.make_async_remote_copy(
-                src_ref=sums.at[level_of(i)],
-                dst_ref=got.at[n_lev - 1 - i],
-                send_sem=sum_sem.at[0, which],
-                recv_sem=sum_sem.at[1, which],
-                device_id=(sec, patch, level_of(i)),
-                device_id_type=MESH,
-            ).start()
-
-    def tracer_a(t, carry):
-        tracer(t, sums_a, t)
-        return carry
-
-    def tracer_b(t, carry):
-        tracer(t, sums_b, t - n_a)
-        return carry
-
-    lax.fori_loop(0, n_a, tracer_a, 0)
-    send_sums(sums_a, got_a, 0)
-    lax.fori_loop(n_a, ntr, tracer_b, 0)
-    send_sums(sums_b, got_b, 1)
+        step1[t, :, 0:LANES] = halo
+        step1[t, :, LANES + ncol : wide] = halo
+        for first in (0, n_tiles - 1):
+            step_1(t, first, 1, rate, rate_vertical)
+            step_2(t, first, 1, rate, rate_vertical, sums, at_row)
+
+    def send_sums(sums, got, which, levels):
+        for d in levels:
+            @pl.when(lev != d)
+            def _(d=d):
+                pltpu.make_async_remote_copy(
+                    src_ref=sums.at[d],
+                    dst_ref=got.at[lax.rem(lev - d + n_lev, n_lev) - 1],
+                    send_sem=sum_sem.at[0, which],
+                    recv_sem=sum_sem.at[1, which],
+                    device_id=(sec, patch, d),
+                    device_id_type=MESH,
+                ).start()
+
+    def all_tracers(step):
+        def with_a(t, carry):
+            step(t, sums_a, t)
+            return carry
+
+        def with_b(t, carry):
+            step(t, sums_b, t - n_a)
+            return carry
+
+        lax.fori_loop(0, n_a, with_a, 0)
+        lax.fori_loop(n_a, ntr, with_b, 0)
+
+    all_tracers(inner)
+    for sums, got, which in ((sums_a, got_a, 0), (sums_b, got_b, 1)):
+        send_sums(sums, got, which, range(1, n_lev - 1))
+
+    pltpu.make_async_copy(edge_recv, edge_recv, edge_sem.at[1]).wait()
+    beside = jnp.where(
+        lane < LANES // 2,
+        pltpu.roll(edge_recv[1, 1], LANES - coef_lane, 1),
+        pltpu.roll(edge_recv[0, 1], LANES - HALO - coef_lane, 1),
+    )
+    total = jnp.zeros((1, LANES), F32)
+    for i in range(4):
+        part = beside[i : i + 1, :]
+        total = total + part
+        for at in (0, LANES + ncol):
+            coef[i, :, at : at + LANES] = jnp.broadcast_to(part, (8, LANES))
+    for at in (0, LANES + ncol):
+        coef[4, :, at : at + LANES] = jnp.broadcast_to(1.0 - total, (8, LANES))
+
+    all_tracers(outer)
+    for sums, got, which in ((sums_a, got_a, 0), (sums_b, got_b, 1)):
+        send_sums(sums, got, which, (0, n_lev - 1))
 
     pick = (
         lax.broadcasted_iota(jnp.int32, (ntr, ntr), 0) == lax.broadcasted_iota(jnp.int32, (ntr, ntr), 1)
@@ -334,7 +356,7 @@
         out = sums[lev]
         for i in range(n_lev - 1):
             out = out + got[i]
-        return out
+        return jnp.concatenate([out[i] for i in range(per_block)], axis=1)
 
     mean_a = level_sums(sums_a, got_a, 0) * (1.0 / alev)
     mixed = jnp.zeros((mixing.shape[0], block), F32)
@@ -422,16 +444,14 @@
     depth = lax.broadcasted_iota(jnp.int32, (nol, block), 0).astype(F32)
     profile = jnp.exp(-depth / 8.0)
     for v in range(2):
-        ocean_v[v] = base_v[v] + profile * forcing[v]
-    pltpu.make_async_copy(ocean_v, ocean_out, out_sem.at[1]).start()
+        ocean_new[v] = base_v[v] + profile * forcing[v]
 
     pltpu.make_async_copy(back_recv, back_recv, back_sem.at[1]).wait()
     at_lane = lax.broadcasted_iota(jnp.int32, (n_patch, LANES), 1)
     own = lax.div(at_lane, slots) == lax.rem(patch, copies)
     returned = jnp.where(own, back_recv[...], 0.0)
     values = jnp.dot(jnp.concatenate(split_2(returned), axis=0), slot_map, preferred_element_type=F32)
-    surface_v[...] = jnp.sum((values[:n_patch] + values[n_patch:]) * hot, axis=0, keepdims=True)
-    pltpu.make_async_copy(surface_v, surface_out, out_sem.at[2]).start()
+    surface_new[...] = jnp.sum((values[:n_patch] + values[n_patch:]) * hot, axis=0, keepdims=True)
 
     six = edge_recv
     pltpu.make_async_copy(six, six, edge_sem.at[0]).wait()
@@ -454,9 +474,14 @@
             some = ref.at[pl.ds(0, count), :]
             pltpu.make_async_copy(some, some, sem.at[0]).wait()
         count //= 2
-    pltpu.make_async_copy(result, atm_out, out_sem.at[0]).wait()
-    pltpu.make_async_copy(ocean_v, ocean_out, out_sem.at[1]).wait()
-    pltpu.make_async_copy(surface_v, surface_out, out_sem.at[2]).wait()
+
+
+def store(a, b, c, a_out, b_out, c_out, sem):
+    copies = [pltpu.make_async_copy(x, y, sem.at[i]) for i, (x, y) in enumerate(((a, a_out), (b, b_out), (c, c_out)))]
+    for copy in copies:
+        copy.start()
+    for copy in copies:
+        copy.wait()
 
 
 def solution(mesh):
@@ -471,7 +496,12 @@
         owners, mask = owners.reshape(1, -1), mask.reshape(1, -1)
         dma = pltpu.SemaphoreType.DMA
         vmem = pltpu.VMEM
-        any_space = pl.BlockSpec(memory_space=pl.ANY)
+        any_space = pl.BlockSpec(memory_space=pltpu.HBM)
+        in_vmem = pl.BlockSpec(memory_space=pltpu.VMEM)
+        operands = [
+            pltpu.with_memory_space_constraint(x, pltpu.HBM)
+            for x in (atm, offs, edge, rates, mixing, owners, weights, mask, ocean, forcing_mix)
+        ]
         out = pl.pallas_call(
             functools.partial(interval, dims),
             out_shape=(
@@ -480,11 +510,10 @@
                 jax.ShapeDtypeStruct((1, block), F32),
             ),
             in_specs=[any_space] * 10,
-            out_specs=(any_space,) * 3,
+            out_specs=(in_vmem,) * 3,
             scratch_shapes=[
                 vmem((ntr, rows, wide), F32),
-                vmem((rows, wide), F32),
-                vmem(atm.shape, F32),
+                vmem((ntr, rows, wide), F32),
                 vmem((5, 8, wide), F32),
                 vmem(offs.shape, jnp.int32),
                 vmem(edge.shape, F32),
@@ -498,15 +527,14 @@
                 vmem(forcing_mix.shape, F32),
                 vmem((2, 8, LANES), F32),
                 vmem((2, 3, 8, LANES), F32),
-                vmem((n_lev, 8, block), F32),
-                vmem((n_lev, ntr - 8, block), F32),
-                vmem((n_lev - 1, 8, block), F32),
-                vmem((n_lev - 1, ntr - 8, block), F32),
+                vmem((n_lev, block // LANES, 8, LANES), F32),
+                vmem((n_lev, block // LANES, ntr - 8, LANES), F32),
+                vmem((n_lev - 1, block // LANES, 8, LANES), F32),
+                vmem((n_lev - 1, block // LANES, ntr - 8, LANES), F32),
                 vmem((n_patch, 2 * LANES), F32),
                 vmem((n_patch, 2 * LANES), F32),
                 vmem((weights.shape[0] // LANES, LANES), F32),
                 vmem((n_patch, LANES), F32),
-                vmem((1, block), F32),
                 vmem((n_patch, block), F32),
                 vmem((LANES, block), BF16),
                 vmem((ntr, nflux, block), F32),
@@ -519,13 +547,20 @@
                 dma((2, 2)),
                 dma((2,)),
                 dma((2,)),
-                dma((3,)),
             ],
             compiler_params=pltpu.CompilerParams(
-                collective_id=0, has_side_effects=True, vmem_limit_bytes=32 * 1024 * 1024
+                collective_id=0, has_side_effects=True, vmem_limit_bytes=40 * 1024 * 1024
             ),
             name="interval",
-        )(atm, offs, edge, rates, mixing, owners, weights, mask, ocean, forcing_mix)
+        )(*operands)
+        out = pl.pallas_call(
+            store,
+            out_shape=tuple(jax.ShapeDtypeStruct(x.shape, F32) for x in out),
+            in_specs=[in_vmem] * 3,
+            out_specs=(any_space,) * 3,
+            scratch_shapes=[dma((3,))],
+            name="store",
+        )(*out)
         return out[0], out[1], out[2].reshape(-1)
 
     in_specs = (

time: 65.2 us -> 54.9 us (0.84)
  the two profiles are of different devices: /device:TPU:1 before, /device:TPU:8 now
where the time goes in v2:
time: 54.9 us; the launch traced here: 54.7 us
  Pallas kernels  51.7 us (94%)
  local copies, waits for them, and re-layouts  2.32 us (4%)
  between operations  0.65 us (1%)
    pallas_call x1, Pallas kernels, per_device(): pl.pallas_call(functools.partial(interval, dims), out_shape=(jax.ShapeDty...  49.2 us
    pallas_call x1, Pallas kernels, per_device(): pl.pallas_call(store, out_shape=tuple((jax.ShapeDtypeStruct(x.shape, F32)...  2.54 us
    unnamed x6, local copies, waits for them, and re-layouts  2.32 us

profile of v2, /device:TPU:8, one launch (start us, length us, event | category | flops | bytes accessed | tf_op | source)
XLA Modules:
  0.0 54.7 jit_solution(10435796761547488210)
XLA Ops:
  0.6 49.2 %interval.1 = (f32[10,16,2048]{2,1,0:T(8,128)S(1)}, f32[2,80,256]{2,1,0:T(8,128)S(1)}, f32[1,256]{1,0:T(1,128)S(1)}) custom-call(f32[10,16,2048]{2,1,0:T(8,128)} %atm.1, s32[3,2048]{1,0:T(4,128)} %offs.1, f32[3,2048]{1,0:T(4,128)} %edge.1, f32[10]{0:T(128)} %rates.1, f32[10,10]{1,0:T(8,128)} %mixing.1, s32[1,256]{1,0:T(1,128)} %bitcast.3, ...), custom_call_target="tpu_custom_call" | custom-call | tf_op jit(solution)/shard_map/interval/pallas_call | solution.py:505
  49.8 0.0 copy-start
  49.8 1.1 %copy-done = f32[10,16,2048]{2,1,0:T(8,128)} copy-done((f32[10,16,2048]{2,1,0:T(8,128)}, f32[10,16,2048]{2,1,0:T(8,128)S(1)}, u32[]{:S(2)}) %copy-start) | copy-done | bytes 1310744
  50.9 0.0 copy-start.1
  50.9 0.7 %copy-done.1 = f32[2,80,256]{2,1,0:T(8,128)} copy-done((f32[2,80,256]{2,1,0:T(8,128)}, f32[2,80,256]{2,1,0:T(8,128)S(1)}, u32[]{:S(2)}) %copy-start.1) | copy-done | bytes 163864
  51.6 0.0 copy-start.2
  51.6 0.6 %copy-done.2 = f32[1,256]{1,0:T(1,128)} copy-done((f32[1,256]{1,0:T(1,128)}, f32[1,256]{1,0:T(1,128)S(1)}, u32[]{:S(2)}) %copy-start.2) | copy-done | bytes 1048
  52.1 2.5 %store.1 = (f32[10,16,2048]{2,1,0:T(8,128)}, f32[2,80,256]{2,1,0:T(8,128)}, f32[1,256]{1,0:T(1,128)}) custom-call(f32[10,16,2048]{2,1,0:T(8,128)} %copy-done, f32[2,80,256]{2,1,0:T(8,128)} %copy-done.1, f32[1,256]{1,0:T(1,128)} %copy-done.2), custom_call_target="tpu_custom_call" | custom-call | tf_op jit(solution)/shard_map/store/pallas_call | solution.py:556
Async XLA Ops:
  49.8 1.1 %copy-start = (f32[10,16,2048]{2,1,0:T(8,128)}, f32[10,16,2048]{2,1,0:T(8,128)S(1)}, u32[]{:S(2)}) copy-start(f32[10,16,2048]{2,1,0:T(8,128)S(1)} %get-tuple-element.9.a) | copy-start | bytes 3932164
  50.9 0.7 %copy-start.1 = (f32[2,80,256]{2,1,0:T(8,128)}, f32[2,80,256]{2,1,0:T(8,128)S(1)}, u32[]{:S(2)}) copy-start(f32[2,80,256]{2,1,0:T(8,128)S(1)} %get-tuple-element.10.b) | copy-start | bytes 491524
  51.6 0.6 %copy-start.2 = (f32[1,256]{1,0:T(1,128)}, f32[1,256]{1,0:T(1,128)S(1)}, u32[]{:S(2)}) copy-start(f32[1,256]{1,0:T(1,128)S(1)} %get-tuple-element.11.c) | copy-start | bytes 3076

commit v3 on v2

--- a/solution.py
+++ b/solution.py
@@ -45,7 +45,9 @@
         other = lax.rem(place + step + n_place, n_place)
         return lax.div(other, n_patch), lax.rem(other, n_patch)
 
-    left, right = column_neighbour(-1), column_neighbour(1)
+    def beside(side):
+        s, p = column_neighbour(2 * side - 1)
+        return s, p, s < sec, s > sec
 
     def level_of(step):
         return lax.rem(lev + step + n_lev, n_lev)
@@ -55,9 +57,16 @@
     def greet(where):
         pl.semaphore_signal(barrier, inc=1, device_id=where, device_id_type=MESH)
 
-    for step in (-1, 0, 1):
-        for s, p in (left, right):
-            greet((s, p, level_of(step)))
+    expected = (n_lev - 1) + (n_patch - 1)
+    for side in range(2):
+        s, p, lower, higher = beside(side)
+
+        @pl.when(jnp.logical_not(lower))
+        def _(s=s, p=p):
+            for step in (-1, 0, 1):
+                greet((s, p, level_of(step)))
+
+        expected = expected + jnp.where(higher, 0, 3)
     for i in range(1, n_lev):
         greet((sec, patch, level_of(i)))
 
@@ -117,18 +126,24 @@
     edge_send[0] = first
     edge_send[1] = last
 
-    pl.semaphore_wait(barrier, 6 + (n_lev - 1) + (n_patch - 1))
-
-    for side, (s, p) in ((0, right), (1, left)):
+    pl.semaphore_wait(barrier, expected)
+
+    def send_edge(side):
+        s, p, _, _ = beside(side)
         for step in (0, -1, 1):
             pltpu.make_async_remote_copy(
-                src_ref=edge_send.at[1 - side],
-                dst_ref=edge_recv.at[side, 1 - step],
+                src_ref=edge_send.at[side],
+                dst_ref=edge_recv.at[1 - side, 1 - step],
                 send_sem=edge_sem.at[0],
-                recv_sem=edge_sem.at[1],
+                recv_sem=edge_sem.at[2 - side],
                 device_id=(s, p, level_of(step)),
                 device_id_type=MESH,
             ).start()
+
+    for side in range(2):
+        @pl.when(jnp.logical_not(beside(side)[3]))
+        def _(side=side):
+            send_edge(side)
 
     def to_lower(t):
         return pltpu.make_async_remote_copy(
@@ -200,19 +215,27 @@
     )
     inside_halo = inside[klev:, :]
 
+    def halo_lane(side):
+        return (1 - side) * (LANES - HALO)
+
+    def halo_at(side):
+        return pl.multiple_of(side * (LANES + ncol), LANES)
+
     def across(x, times):
         return jnp.concatenate([x] * times, axis=1) if times > 1 else x
 
     def down(x):
         return jnp.concatenate([x] * (rows // 8), axis=0)
 
-    def stencil(x, at, tiles, rate, rate_vertical):
+    def stencil(x, at, first, tiles, rate, rate_vertical):
         width = tiles * LANES
-        middle = x[:, LANES : LANES + width]
-        out = middle * (down(coef[4, :, at : at + width]) - across(rate_vertical, tiles))
+        part = slice(first * LANES, first * LANES + width)
+        middle = x[:, part]
+        columns = pl.ds(at, width)
+        out = middle * (down(coef[4, :, columns]) - across(rate_vertical, tiles))
         for i, delta in enumerate(DELTAS):
-            moved = pltpu.roll(x, (-delta) % x.shape[1], 1)[:, LANES : LANES + width]
-            out = out + down(coef[i, :, at : at + width]) * moved
+            moved = pltpu.roll(x, (-delta) % x.shape[1], 1)[:, part]
+            out = out + down(coef[i, :, columns]) * moved
         one = pltpu.roll(middle, 1, 0) + pltpu.roll(middle, rows - 1, 0)
         two = pltpu.roll(middle, 2, 0) + pltpu.roll(middle, rows - 2, 0)
         return out + rate * (one + 0.5 * two)
@@ -229,12 +252,12 @@
     def step_1(t, first, tiles, rate, rate_vertical):
         at = LANES * (1 + first)
         x = ring[t, :, at - LANES : at + (tiles + 1) * LANES]
-        step1[t, :, at : at + tiles * LANES] = masked(stencil(x, at, tiles, rate, rate_vertical), tiles)
+        step1[:, at : at + tiles * LANES] = masked(stencil(x, at, 1, tiles, rate, rate_vertical), tiles)
 
     def step_2(t, first, tiles, rate, rate_vertical, sums, at_row):
         at = LANES * (1 + first)
-        x = step1[t, :, at - LANES : at + (tiles + 1) * LANES]
-        out = stencil(x, at, tiles, rate, rate_vertical)[:klev]
+        x = step1[:, at - LANES : at + (tiles + 1) * LANES]
+        out = stencil(x, at, 1, tiles, rate, rate_vertical)[:klev]
         result[t, :, at - LANES : at + (tiles - 1) * LANES] = out
         column_sums = jnp.sum(out, axis=0, keepdims=True)
         for i in range(tiles):
@@ -258,46 +281,34 @@
             low, high = max(first, 1), min(first + 4, n_tiles - 1)
             step_2(t, low, high - low, rate, rate_vertical, sums, at_row)
 
-    def outer(t, sums, at_row):
+    def outer(side, t, sums, at_row):
         rate = rates_s[t]
         rate_vertical = rate * vertical
         low, high = 2 * HALO * t, 2 * HALO * t + HALO
 
-        def sides(from_left, from_right, lanes_at):
-            return jnp.where(
-                lane < LANES // 2,
-                pltpu.roll(from_right, lax.rem(LANES - lanes_at, LANES), 1),
-                pltpu.roll(from_left, LANES - HALO - lanes_at, 1),
-            )
-
-        corner = jnp.where(
-            row < HALO,
-            sides(edge_recv[0, 2], edge_recv[1, 2], low),
-            sides(edge_recv[0, 0], edge_recv[1, 0], high),
-        )
+        def moved(level, lanes_at):
+            return pltpu.roll(edge_recv[side, level], lax.rem(halo_lane(side) - lanes_at + LANES, LANES), 1)
+
         halo = jnp.concatenate(
             [
-                sides(edge_recv[0, 1], edge_recv[1, 1], low),
-                sides(edge_recv[0, 1], edge_recv[1, 1], high),
-                jnp.where(inside_halo, corner, 0.0),
+                moved(1, low),
+                moved(1, high),
+                jnp.where(inside_halo, jnp.where(row < HALO, moved(2, low), moved(0, high)), 0.0),
             ],
             axis=0,
         )
-        ring[t, :, 0:LANES] = halo
-        ring[t, :, LANES + ncol : wide] = halo
-
-        x = jnp.concatenate([ring[t, :, ncol : ncol + LANES], halo, ring[t, :, LANES : 2 * LANES]], axis=1)
-        halo = masked(stencil(x, 0, 1, rate, rate_vertical), 1)
-        step1[t, :, 0:LANES] = halo
-        step1[t, :, LANES + ncol : wide] = halo
-        for first in (0, n_tiles - 1):
-            step_1(t, first, 1, rate, rate_vertical)
-            step_2(t, first, 1, rate, rate_vertical, sums, at_row)
-
-    def send_sums(sums, got, which, levels):
-        for d in levels:
-            @pl.when(lev != d)
-            def _(d=d):
+        ring[t, :, pl.ds(halo_at(side), LANES)] = halo
+        start = pl.multiple_of(side * (wide - 3 * LANES), LANES)
+        x = ring[t, :, pl.ds(start, 3 * LANES)]
+        x = masked(stencil(x, start, 0, 3, rate, rate_vertical), 3)
+        out = stencil(x, pl.multiple_of(start + LANES, LANES), 1, 1, rate, rate_vertical)[:klev]
+        result[t, :, pl.ds(pl.multiple_of(side * (ncol - LANES), LANES), LANES)] = out
+        sums[side * (n_lev - 1), side * (per_block - 1), pl.ds(at_row, 1), :] = jnp.sum(out, axis=0, keepdims=True)
+
+    def send_sums(d):
+        @pl.when(lev != d)
+        def _():
+            for which, (sums, got) in enumerate(((sums_a, got_a), (sums_b, got_b))):
                 pltpu.make_async_remote_copy(
                     src_ref=sums.at[d],
                     dst_ref=got.at[lax.rem(lev - d + n_lev, n_lev) - 1],
@@ -320,27 +331,31 @@
         lax.fori_loop(n_a, ntr, with_b, 0)
 
     all_tracers(inner)
-    for sums, got, which in ((sums_a, got_a, 0), (sums_b, got_b, 1)):
-        send_sums(sums, got, which, range(1, n_lev - 1))
-
-    pltpu.make_async_copy(edge_recv, edge_recv, edge_sem.at[1]).wait()
-    beside = jnp.where(
-        lane < LANES // 2,
-        pltpu.roll(edge_recv[1, 1], LANES - coef_lane, 1),
-        pltpu.roll(edge_recv[0, 1], LANES - HALO - coef_lane, 1),
-    )
-    total = jnp.zeros((1, LANES), F32)
-    for i in range(4):
-        part = beside[i : i + 1, :]
-        total = total + part
-        for at in (0, LANES + ncol):
-            coef[i, :, at : at + LANES] = jnp.broadcast_to(part, (8, LANES))
-    for at in (0, LANES + ncol):
-        coef[4, :, at : at + LANES] = jnp.broadcast_to(1.0 - total, (8, LANES))
-
-    all_tracers(outer)
-    for sums, got, which in ((sums_a, got_a, 0), (sums_b, got_b, 1)):
-        send_sums(sums, got, which, (0, n_lev - 1))
+    for d in range(1, n_lev - 1):
+        send_sums(d)
+
+    def one_side(i, carry):
+        side = lax.rem(i + (patch == 0).astype(jnp.int32), 2)
+        here = edge_recv.at[side]
+        pltpu.make_async_copy(here, here, edge_sem.at[1 + side]).wait()
+
+        @pl.when(beside(side)[3])
+        def _():
+            send_edge(side)
+
+        around = pltpu.roll(edge_recv[side, 1], lax.rem(halo_lane(side) - coef_lane + LANES, LANES), 1)
+        total = jnp.zeros((1, LANES), F32)
+        columns = pl.ds(halo_at(side), LANES)
+        for k in range(4):
+            part = around[k : k + 1, :]
+            total = total + part
+            coef[k, :, columns] = jnp.broadcast_to(part, (8, LANES))
+        coef[4, :, columns] = jnp.broadcast_to(1.0 - total, (8, LANES))
+        all_tracers(functools.partial(outer, side))
+        send_sums(side * (n_lev - 1))
+        return carry
+
+    lax.fori_loop(0, 2, one_side, 0)
 
     pick = (
         lax.broadcasted_iota(jnp.int32, (ntr, ntr), 0) == lax.broadcasted_iota(jnp.int32, (ntr, ntr), 1)
@@ -453,8 +468,7 @@
     values = jnp.dot(jnp.concatenate(split_2(returned), axis=0), slot_map, preferred_element_type=F32)
     surface_new[...] = jnp.sum((values[:n_patch] + values[n_patch:]) * hot, axis=0, keepdims=True)
 
-    six = edge_recv
-    pltpu.make_async_copy(six, six, edge_sem.at[0]).wait()
+    pltpu.make_async_copy(edge_recv, edge_recv, edge_sem.at[0]).wait()
 
     @pl.when(lev > 0)
     def _():
@@ -513,7 +527,7 @@
             out_specs=(in_vmem,) * 3,
             scratch_shapes=[
                 vmem((ntr, rows, wide), F32),
-                vmem((ntr, rows, wide), F32),
+                vmem((rows, wide), F32),
                 vmem((5, 8, wide), F32),
                 vmem(offs.shape, jnp.int32),
                 vmem(edge.shape, F32),
@@ -540,7 +554,7 @@
                 vmem((ntr, nflux, block), F32),
                 dma((ntr,)),
                 dma((9,)),
-                dma((2,)),
+                dma((3,)),
                 dma((2, ntr)),
                 dma((ntr,)),
                 dma((ntr,)),
@@ -559,6 +573,7 @@
             in_specs=[in_vmem] * 3,
             out_specs=(any_space,) * 3,
             scratch_shapes=[dma((3,))],
+            compiler_params=pltpu.CompilerParams(vmem_limit_bytes=8 * 1024 * 1024),
             name="store",
         )(*out)
         return out[0], out[1], out[2].reshape(-1)

time: 54.9 us -> 49.7 us (0.905)
  Pallas kernels: 51.7 us -> 48.8 us
  local copies, waits for them, and re-layouts: 2.32 us -> 0 us
    unnamed x6 -> x0, local copies, waits for them, and re-layouts: 2.32 us -> none
    pallas_call x1, Pallas kernels: 49.2 us -> 47.7 us  [per_device(): pl.pallas_call(functools.partial(interval, dims), out_shape=(jax.ShapeDty...]
    pallas_call x1, Pallas kernels: 2.54 us -> 1.13 us  [per_device(): pl.pallas_call(store, out_shape=tuple((jax.ShapeDtypeStruct(x.shape, F32)...]
where the time goes in v3:
time: 49.7 us; the launch traced here: 49.5 us
  Pallas kernels  48.8 us (98%)
  between operations  0.64 us (1%)
    pallas_call x1, Pallas kernels, per_device(): pl.pallas_call(functools.partial(interval, dims), out_shape=(jax.ShapeDty...  47.7 us
    pallas_call x1, Pallas kernels, per_device(): pl.pallas_call(store, out_shape=tuple((jax.ShapeDtypeStruct(x.shape, F32)...  1.13 us

profile of v3, /device:TPU:8, one launch (start us, length us, event | category | flops | bytes accessed | tf_op | source)
XLA Modules:
  0.0 49.5 jit_solution(6268865368938802108)
XLA Ops:
  0.6 47.7 %interval.1 = (f32[10,16,2048]{2,1,0:T(8,128)S(1)}, f32[2,80,256]{2,1,0:T(8,128)S(1)}, f32[1,256]{1,0:T(1,128)S(1)}) custom-call(f32[10,16,2048]{2,1,0:T(8,128)} %atm.1, s32[3,2048]{1,0:T(4,128)} %offs.1, f32[3,2048]{1,0:T(4,128)} %edge.1, f32[10]{0:T(128)} %rates.1, f32[10,10]{1,0:T(8,128)} %mixing.1, s32[1,256]{1,0:T(1,128)} %bitcast.3, ...), custom_call_target="tpu_custom_call" | custom-call | tf_op jit(solution)/shard_map/interval/pallas_call | solution.py:519
  48.3 1.1 %store.1 = (f32[10,16,2048]{2,1,0:T(8,128)}, f32[2,80,256]{2,1,0:T(8,128)}, f32[1,256]{1,0:T(1,128)}) custom-call(f32[10,16,2048]{2,1,0:T(8,128)S(1)} %get-tuple-element.9.a, f32[2,80,256]{2,1,0:T(8,128)S(1)} %get-tuple-element.10.b, f32[1,256]{1,0:T(1,128)S(1)} %get-tuple-element.11.c), custom_call_target="tpu_custom_call" | custom-call | tf_op jit(solution)/shard_map/store/pallas_call | solution.py:570

commit v4 on v3

--- a/solution.py
+++ b/solution.py
@@ -26,7 +26,7 @@
     ring, step1, coef, offs_v, edge_v, rates_s, mix_v, owners_v, weights_v, mask_v, ocean_v, base_v, fmix_v,
     edge_send, edge_recv, sums_a, sums_b, got_a, got_b, flux_send, flux_recv, back_send, back_recv,
     cols_hot, slot_hot, mix_cols,
-    atm_sem, in_sem, edge_sem, lev_send_sem, lev_up_sem, lev_down_sem, sum_sem, flux_sem, back_sem,
+    atm_sem, in_sem, edge_sem, answer_sem, lev_send_sem, lev_up_sem, lev_down_sem, sum_sem, flux_sem, back_sem,
 ):
     n_sec, n_patch, n_lev = dims
     ntr, klev, ncol = atm.shape
@@ -57,21 +57,35 @@
     def greet(where):
         pl.semaphore_signal(barrier, inc=1, device_id=where, device_id_type=MESH)
 
-    expected = (n_lev - 1) + (n_patch - 1)
+    first_opens = (sec > 0).astype(jnp.int32)
+    last_opens = (sec == n_sec - 1).astype(jnp.int32) if n_sec > 1 else jnp.int32(0)
+
+    def opens(p):
+        return ((p == 0) & (first_opens == 1)) | ((p == n_patch - 1) & (last_opens == 1))
+
+    opener = opens(patch)
+    openers_beside = first_opens * last_opens
+    expected = (n_lev - 1) + jnp.where(opener, openers_beside, n_patch - 1)
     for side in range(2):
         s, p, lower, higher = beside(side)
-
-        @pl.when(jnp.logical_not(lower))
+        same = jnp.logical_not(lower | higher)
+
+        @pl.when(higher | (same & (opener | jnp.logical_not(opens(p)))))
         def _(s=s, p=p):
             for step in (-1, 0, 1):
                 greet((s, p, level_of(step)))
 
-        expected = expected + jnp.where(higher, 0, 3)
+        expected = expected + jnp.where(lower | (same & jnp.logical_not(opener)), 3, 0)
     for i in range(1, n_lev):
         greet((sec, patch, level_of(i)))
 
     def greet_patch(i, carry):
-        greet((sec, lax.rem(patch + i, n_patch), lev))
+        other = lax.rem(patch + i, n_patch)
+
+        @pl.when(opener | jnp.logical_not(opens(other)))
+        def _():
+            greet((sec, other, lev))
+
         return carry
 
     lax.fori_loop(1, n_patch, greet_patch, 0)
@@ -140,10 +154,26 @@
                 device_id_type=MESH,
             ).start()
 
+    def answer(where):
+        pl.semaphore_signal(answer_sem, inc=1, device_id=where, device_id_type=MESH)
+
     for side in range(2):
-        @pl.when(jnp.logical_not(beside(side)[3]))
+        s, p, lower, higher = beside(side)
+        same = jnp.logical_not(lower | higher)
+
+        @pl.when(lower | (same & jnp.logical_not(opener)))
         def _(side=side):
             send_edge(side)
+
+        @pl.when(same & jnp.logical_not(opener) & opens(p))
+        def _(s=s, p=p):
+            for step in (-1, 0, 1):
+                answer((s, p, level_of(step)))
+
+    for p in (0, n_patch - 1):
+        @pl.when(jnp.logical_not(opener) & opens(jnp.int32(p)))
+        def _(p=p):
+            answer((sec, p, lev))
 
     def to_lower(t):
         return pltpu.make_async_remote_copy(
@@ -204,6 +234,16 @@
     above = jnp.where(level < nol - 1, pltpu.roll(state, nol - 1, 1) - state, 0.0)
     below = jnp.where(level > 0, pltpu.roll(state, 1, 1) - state, 0.0)
     base_v[...] = state + 0.2 * above + 0.2 * below
+
+    @pl.when(opener)
+    def _():
+        pl.semaphore_wait(answer_sem, n_patch - 1 - openers_beside + 3)
+        for side in range(2):
+            _, _, lower, higher = beside(side)
+
+            @pl.when(jnp.logical_not(lower | higher))
+            def _(side=side):
+                send_edge(side)
 
     ring_row = lax.broadcasted_iota(jnp.int32, (rows, LANES), 0)
     k = lev * klev + jnp.where(ring_row < klev + HALO, ring_row, ring_row - rows)
@@ -394,8 +434,20 @@
     for v in range(2):
         flux_send[:, v * LANES : (v + 1) * LANES] = outgoing[v]
 
+    across_patch = 4
+    down_patch = n_patch // across_patch
+
+    def far_first(i):
+        def moved(i, n):
+            half = lax.div(i + 1, 2)
+            return n // 2 + jnp.where(lax.rem(i, 2) == 1, -half, half)
+
+        y = lax.div(patch, across_patch) + moved(lax.div(i, across_patch), down_patch)
+        x = lax.rem(patch, across_patch) + moved(lax.rem(i, across_patch), across_patch)
+        return lax.rem(y, down_patch) * across_patch + lax.rem(x, across_patch)
+
     def send_flux(i, carry):
-        other = lax.rem(patch + i, n_patch)
+        other = far_first(i)
         pltpu.make_async_remote_copy(
             src_ref=flux_send.at[pl.ds(other, 1), :],
             dst_ref=flux_recv.at[pl.ds(patch, 1), :],
@@ -406,7 +458,7 @@
         ).start()
         return carry
 
-    lax.fori_loop(1, n_patch, send_flux, 0)
+    lax.fori_loop(0, n_patch - 1, send_flux, 0)
     own_row = pl.ds(patch, 1)
     pltpu.make_async_copy(flux_send.at[own_row, :], flux_recv.at[own_row, :], flux_sem.at[1]).start()
     ocean_cells = mask_v[...].astype(F32)
@@ -440,7 +492,7 @@
         back_send[g : g + 1, :] = back[:, g * LANES : (g + 1) * LANES]
 
     def send_back(i, carry):
-        other = lax.rem(patch + i, n_patch)
+        other = far_first(i)
         pltpu.make_async_remote_copy(
             src_ref=back_send.at[pl.ds(lax.div(other, copies), 1), :],
             dst_ref=back_recv.at[pl.ds(patch, 1), :],
@@ -451,7 +503,7 @@
         ).start()
         return carry
 
-    lax.fori_loop(1, n_patch, send_back, 0)
+    lax.fori_loop(0, n_patch - 1, send_back, 0)
     pltpu.make_async_copy(
         back_send.at[pl.ds(lax.div(patch, copies), 1), :], back_recv.at[own_row, :], back_sem.at[1]
     ).start()
@@ -555,6 +607,7 @@
                 dma((ntr,)),
                 dma((9,)),
                 dma((3,)),
+                pltpu.SemaphoreType.REGULAR,
                 dma((2, ntr)),
                 dma((ntr,)),
                 dma((ntr,)),

time: 49.7 us -> 47.9 us (0.964)
  Pallas kernels: 48.8 us -> 47.1 us
    pallas_call x1, Pallas kernels: 47.7 us -> 46 us  [per_device(): pl.pallas_call(functools.partial(interval, dims), out_shape=(jax.ShapeDty...]
where the time goes in v4:
time: 47.9 us; the launch traced here: 47.7 us
  Pallas kernels  47.1 us (98%)
  between operations  0.64 us (1%)
    pallas_call x1, Pallas kernels, per_device(): pl.pallas_call(functools.partial(interval, dims), out_shape=(jax.ShapeDty...  46 us
    pallas_call x1, Pallas kernels, per_device(): pl.pallas_call(store, out_shape=tuple((jax.ShapeDtypeStruct(x.shape, F32)...  1.13 us

profile of v4, /device:TPU:8, one launch (start us, length us, event | category | flops | bytes accessed | tf_op | source)
XLA Modules:
  0.0 47.7 jit_solution(9115606760758298263)
XLA Ops:
  0.6 46.0 %interval.1 = (f32[10,16,2048]{2,1,0:T(8,128)S(1)}, f32[2,80,256]{2,1,0:T(8,128)S(1)}, f32[1,256]{1,0:T(1,128)S(1)}) custom-call(f32[10,16,2048]{2,1,0:T(8,128)} %atm.1, s32[3,2048]{1,0:T(4,128)} %offs.1, f32[3,2048]{1,0:T(4,128)} %edge.1, f32[10]{0:T(128)} %rates.1, f32[10,10]{1,0:T(8,128)} %mixing.1, s32[1,256]{1,0:T(1,128)} %bitcast.3, ...), custom_call_target="tpu_custom_call" | custom-call | tf_op jit(solution)/shard_map/interval/pallas_call | solution.py:571
  46.6 1.1 %store.1 = (f32[10,16,2048]{2,1,0:T(8,128)}, f32[2,80,256]{2,1,0:T(8,128)}, f32[1,256]{1,0:T(1,128)}) custom-call(f32[10,16,2048]{2,1,0:T(8,128)S(1)} %get-tuple-element.9.a, f32[2,80,256]{2,1,0:T(8,128)S(1)} %get-tuple-element.10.b, f32[1,256]{1,0:T(1,128)S(1)} %get-tuple-element.11.c), custom_call_target="tpu_custom_call" | custom-call | tf_op jit(solution)/shard_map/store/pallas_call | solution.py:623

commit v5 on v4

--- a/solution.py
+++ b/solution.py
@@ -12,6 +12,7 @@
 DELTAS = (-2, -1, 1, 2)
 LANES = 128
 HALO = 4
+GROUP = 3 * HALO
 
 
 def split_2(x):
@@ -24,7 +25,7 @@
     atm, offs, edge, rates, mixing, owners, weights, mask, ocean, forcing_mix,
     result, ocean_new, surface_new,
     ring, step1, coef, offs_v, edge_v, rates_s, mix_v, owners_v, weights_v, mask_v, ocean_v, base_v, fmix_v,
-    edge_send, edge_recv, sums_a, sums_b, got_a, got_b, flux_send, flux_recv, back_send, back_recv,
+    edge_send, edge_recv, own_edge, outer_v, sums_a, sums_b, got_a, got_b, flux_send, flux_recv, back_send, back_recv,
     cols_hot, slot_hot, mix_cols,
     atm_sem, in_sem, edge_sem, answer_sem, lev_send_sem, lev_up_sem, lev_down_sem, sum_sem, flux_sem, back_sem,
 ):
@@ -118,27 +119,37 @@
 
     lane = lax.broadcasted_iota(jnp.int32, (8, LANES), 1)
     row = lax.broadcasted_iota(jnp.int32, (8, LANES), 0)
-    coef_lane = 2 * ntr * HALO
     for load in atm_loads:
         load.wait()
-    first = jnp.zeros((8, LANES), F32)
-    last = jnp.zeros((8, LANES), F32)
-    for t in range(ntr):
-        for k in range(2):
-            at = (2 * t + k) * HALO
-            here = (lane >= at) & (lane < at + HALO)
-            a = ring[t, 8 * k : 8 * k + 8, LANES : 2 * LANES]
-            b = ring[t, 8 * k : 8 * k + 8, ncol : ncol + LANES]
-            first = jnp.where(here, pltpu.roll(a, at, 1) if at else a, first)
-            last = jnp.where(here, pltpu.roll(b, at + HALO, 1), last)
-    here = (lane >= coef_lane) & (lane < coef_lane + HALO)
-    for i in range(4):
-        a = coef[i, :, LANES : 2 * LANES]
-        b = coef[i, :, ncol : ncol + LANES]
-        first = jnp.where(here & (row == i), pltpu.roll(a, coef_lane, 1), first)
-        last = jnp.where(here & (row == i), pltpu.roll(b, coef_lane + HALO, 1), last)
-    edge_send[0] = first
-    edge_send[1] = last
+
+    def packed(of_tracer, source, width, target):
+        out = jnp.zeros((8, LANES), F32)
+        for t in range(ntr):
+            at = GROUP * t + target
+            shift = (at - source) % LANES
+            x = of_tracer(t)
+            out = jnp.where((lane >= at) & (lane < at + width), pltpu.roll(x, shift, 1) if shift else x, out)
+        return out
+
+    starts = (LANES, ncol)
+    coef_rows = []
+    for start in starts:
+        out = jnp.zeros((8, LANES), F32)
+        for i in range(4):
+            out = jnp.where(row == i, coef[i, :, start : start + LANES], out)
+        coef_rows.append(out)
+
+    def at_border(side, k, source, width, target):
+        if k == 3:
+            return packed(lambda t: coef_rows[side], source, width, target)
+        start = starts[side]
+        return packed(lambda t: ring[t, 8 * k : 8 * k + 8, start : start + LANES], source, width, target)
+
+    for i, k in enumerate((0, 1, 3)):
+        edge_send[0, i] = at_border(0, k, 0, HALO, 2 * HALO)
+        edge_send[1, i] = at_border(1, k, LANES - HALO, HALO, 0)
+    own_edge[0, 3] = at_border(0, 3, 0, 2 * HALO, HALO)
+    own_edge[1, 3] = at_border(1, 3, LANES - 2 * HALO, 2 * HALO, 0)
 
     pl.semaphore_wait(barrier, expected)
 
@@ -255,27 +266,17 @@
     )
     inside_halo = inside[klev:, :]
 
-    def halo_lane(side):
-        return (1 - side) * (LANES - HALO)
-
-    def halo_at(side):
-        return pl.multiple_of(side * (LANES + ncol), LANES)
-
     def across(x, times):
         return jnp.concatenate([x] * times, axis=1) if times > 1 else x
 
     def down(x):
         return jnp.concatenate([x] * (rows // 8), axis=0)
 
-    def stencil(x, at, first, tiles, rate, rate_vertical):
-        width = tiles * LANES
-        part = slice(first * LANES, first * LANES + width)
+    def stencil(x, part, centre, sides, rate):
         middle = x[:, part]
-        columns = pl.ds(at, width)
-        out = middle * (down(coef[4, :, columns]) - across(rate_vertical, tiles))
-        for i, delta in enumerate(DELTAS):
-            moved = pltpu.roll(x, (-delta) % x.shape[1], 1)[:, part]
-            out = out + down(coef[i, :, columns]) * moved
+        out = middle * centre
+        for side, delta in zip(sides, DELTAS):
+            out = out + side * pltpu.roll(x, (-delta) % x.shape[1], 1)[:, part]
         one = pltpu.roll(middle, 1, 0) + pltpu.roll(middle, rows - 1, 0)
         two = pltpu.roll(middle, 2, 0) + pltpu.roll(middle, rows - 2, 0)
         return out + rate * (one + 0.5 * two)
@@ -285,24 +286,20 @@
             [x[:klev], jnp.where(across(inside_halo, tiles), x[klev:], 0.0)], axis=0
         )
 
-    n_tiles = ncol // LANES
     per_block = block // LANES
     n_a = sums_a.shape[2]
-
-    def step_1(t, first, tiles, rate, rate_vertical):
-        at = LANES * (1 + first)
-        x = ring[t, :, at - LANES : at + (tiles + 1) * LANES]
-        step1[:, at : at + tiles * LANES] = masked(stencil(x, at, 1, tiles, rate, rate_vertical), tiles)
-
-    def step_2(t, first, tiles, rate, rate_vertical, sums, at_row):
-        at = LANES * (1 + first)
-        x = step1[:, at - LANES : at + (tiles + 1) * LANES]
-        out = stencil(x, at, 1, tiles, rate, rate_vertical)[:klev]
-        result[t, :, at - LANES : at + (tiles - 1) * LANES] = out
-        column_sums = jnp.sum(out, axis=0, keepdims=True)
-        for i in range(tiles):
-            d, half = divmod(first + i, per_block)
-            sums[d, half, pl.ds(at_row, 1), :] = column_sums[:, i * LANES : (i + 1) * LANES]
+    tiles = 8
+    chunk = tiles * LANES
+
+    def step(x, at, rate, rate_vertical):
+        columns = slice(at, at + chunk)
+        return stencil(
+            x,
+            slice(LANES, LANES + chunk),
+            down(coef[4, :, columns]) - across(rate_vertical, tiles),
+            [down(coef[i, :, columns]) for i in range(4)],
+            rate,
+        )
 
     def inner(t, sums, at_row):
         @pl.when(lev < n_lev - 1)
@@ -315,35 +312,17 @@
 
         rate = rates_s[t]
         rate_vertical = rate * vertical
-        for first in range(0, n_tiles, 4):
-            step_1(t, first, 4, rate, rate_vertical)
-        for first in range(0, n_tiles, 4):
-            low, high = max(first, 1), min(first + 4, n_tiles - 1)
-            step_2(t, low, high - low, rate, rate_vertical, sums, at_row)
-
-    def outer(side, t, sums, at_row):
-        rate = rates_s[t]
-        rate_vertical = rate * vertical
-        low, high = 2 * HALO * t, 2 * HALO * t + HALO
-
-        def moved(level, lanes_at):
-            return pltpu.roll(edge_recv[side, level], lax.rem(halo_lane(side) - lanes_at + LANES, LANES), 1)
-
-        halo = jnp.concatenate(
-            [
-                moved(1, low),
-                moved(1, high),
-                jnp.where(inside_halo, jnp.where(row < HALO, moved(2, low), moved(0, high)), 0.0),
-            ],
-            axis=0,
-        )
-        ring[t, :, pl.ds(halo_at(side), LANES)] = halo
-        start = pl.multiple_of(side * (wide - 3 * LANES), LANES)
-        x = ring[t, :, pl.ds(start, 3 * LANES)]
-        x = masked(stencil(x, start, 0, 3, rate, rate_vertical), 3)
-        out = stencil(x, pl.multiple_of(start + LANES, LANES), 1, 1, rate, rate_vertical)[:klev]
-        result[t, :, pl.ds(pl.multiple_of(side * (ncol - LANES), LANES), LANES)] = out
-        sums[side * (n_lev - 1), side * (per_block - 1), pl.ds(at_row, 1), :] = jnp.sum(out, axis=0, keepdims=True)
+        for at in range(LANES, LANES + ncol, chunk):
+            x = ring[t, :, at - LANES : at + chunk + LANES]
+            step1[:, at : at + chunk] = masked(step(x, at, rate, rate_vertical), tiles)
+        for at in range(LANES, LANES + ncol, chunk):
+            x = step1[:, at - LANES : at + chunk + LANES]
+            out = step(x, at, rate, rate_vertical)[:klev]
+            result[t, :, at - LANES : at - LANES + chunk] = out
+            column_sums = jnp.sum(out, axis=0, keepdims=True)
+            for i in range(tiles):
+                d, half = divmod(at // LANES - 1 + i, per_block)
+                sums[d, half, pl.ds(at_row, 1), :] = column_sums[:, i * LANES : (i + 1) * LANES]
 
     def send_sums(d):
         @pl.when(lev != d)
@@ -374,6 +353,18 @@
     for d in range(1, n_lev - 1):
         send_sums(d)
 
+    for k in range(3):
+        own_edge[0, k] = at_border(0, k, 0, 2 * HALO, HALO)
+        own_edge[1, k] = at_border(1, k, LANES - 2 * HALO, 2 * HALO, 0)
+    in_group = lane
+    lane_rate = jnp.zeros((8, LANES), F32)
+    for t in range(ntr):
+        here = lane >= GROUP * t
+        in_group = jnp.where(here, lane - GROUP * t, in_group)
+        lane_rate = jnp.where(here, rates_s[t], lane_rate)
+    lane_rate = down(lane_rate)
+    lane_vertical = lane_rate * vertical
+
     def one_side(i, carry):
         side = lax.rem(i + (patch == 0).astype(jnp.int32), 2)
         here = edge_recv.at[side]
@@ -383,19 +374,48 @@
         def _():
             send_edge(side)
 
-        around = pltpu.roll(edge_recv[side, 1], lax.rem(halo_lane(side) - coef_lane + LANES, LANES), 1)
-        total = jnp.zeros((1, LANES), F32)
-        columns = pl.ds(halo_at(side), LANES)
-        for k in range(4):
-            part = around[k : k + 1, :]
-            total = total + part
-            coef[k, :, columns] = jnp.broadcast_to(part, (8, LANES))
-        coef[4, :, columns] = jnp.broadcast_to(1.0 - total, (8, LANES))
-        all_tracers(functools.partial(outer, side))
-        send_sums(side * (n_lev - 1))
+        theirs = (in_group < HALO * (1 - side)) | (in_group >= GROUP - HALO * side)
+        corner = jnp.where(row < HALO, edge_recv[side, 2, 0], edge_recv[side, 0, 1])
+        x = jnp.concatenate(
+            [
+                jnp.where(theirs, edge_recv[side, 1, 0], own_edge[side, 0]),
+                jnp.where(theirs, edge_recv[side, 1, 1], own_edge[side, 1]),
+                jnp.where(inside_halo, jnp.where(theirs, corner, own_edge[side, 2]), 0.0),
+            ],
+            axis=0,
+        )
+        factors = jnp.where(theirs, edge_recv[side, 1, 2], own_edge[side, 3])
+        sides = [factors[k : k + 1, :] for k in range(4)]
+        centre = 1.0 - (sides[0] + sides[1] + sides[2] + sides[3]) - lane_vertical
+        for last in (False, True):
+            x = stencil(x, slice(0, LANES), centre, sides, lane_rate)
+            if not last:
+                x = masked(x, 1)
+        out = x[:klev]
+        outer_v[side] = out
+        column_sums = jnp.broadcast_to(jnp.sum(out, axis=0, keepdims=True), (8, LANES))
+        first_lane = side * (LANES - HALO)
+        changed = (lane >= first_lane) & (lane < first_lane + HALO)
+        d, half = side * (n_lev - 1), side * (per_block - 1)
+        for sums, t0, t1 in ((sums_a, 0, n_a), (sums_b, n_a, ntr)):
+            values = jnp.zeros((8, LANES), F32)
+            for t in range(t0, t1):
+                values = jnp.where(row == t - t0, pltpu.roll(column_sums, (-GROUP * t - HALO) % LANES, 1), values)
+            values = jnp.where(changed, pltpu.roll(values, first_lane, 1), 0.0)
+            sums[d, half] = jnp.where(changed[: t1 - t0], values[: t1 - t0], sums[d, half])
+        send_sums(d)
         return carry
 
     lax.fori_loop(0, 2, one_side, 0)
+    lane_of_two = lax.broadcasted_iota(jnp.int32, (klev, LANES), 1)
+    for side in range(2):
+        out = outer_v[side]
+        first_lane = side * (LANES - HALO)
+        changed = (lane_of_two >= first_lane) & (lane_of_two < first_lane + HALO)
+        columns = slice(side * (ncol - LANES), side * (ncol - LANES) + LANES)
+        for t in range(ntr):
+            shift = (first_lane - GROUP * t - HALO) % LANES
+            result[t, :, columns] = jnp.where(changed, pltpu.roll(out, shift, 1), result[t, :, columns])
 
     pick = (
         lax.broadcasted_iota(jnp.int32, (ntr, ntr), 0) == lax.broadcasted_iota(jnp.int32, (ntr, ntr), 1)
@@ -591,8 +611,10 @@
                 vmem(ocean.shape, F32),
                 vmem(ocean.shape, F32),
                 vmem(forcing_mix.shape, F32),
-                vmem((2, 8, LANES), F32),
                 vmem((2, 3, 8, LANES), F32),
+                vmem((2, 3, 3, 8, LANES), F32),
+                vmem((2, 4, 8, LANES), F32),
+                vmem((2, klev, LANES), F32),
                 vmem((n_lev, block // LANES, 8, LANES), F32),
                 vmem((n_lev, block // LANES, ntr - 8, LANES), F32),
                 vmem((n_lev - 1, block // LANES, 8, LANES), F32),

time: 47.9 us -> 47.2 us (0.985)
  Pallas kernels: 47.1 us -> 46.4 us
    pallas_call x1, Pallas kernels: 46 us -> 45.3 us  [per_device(): pl.pallas_call(functools.partial(interval, dims), out_shape=(jax.ShapeDty...]
where the time goes in v5:
time: 47.2 us; the launch traced here: 47 us
  Pallas kernels  46.4 us (98%)
  between operations  0.64 us (1%)
    pallas_call x1, Pallas kernels, per_device(): pl.pallas_call(functools.partial(interval, dims), out_shape=(jax.ShapeDty...  45.3 us
    pallas_call x1, Pallas kernels, per_device(): pl.pallas_call(store, out_shape=tuple((jax.ShapeDtypeStruct(x.shape, F32)...  1.13 us

profile of v5, /device:TPU:8, one launch (start us, length us, event | category | flops | bytes accessed | tf_op | source)
XLA Modules:
  0.0 47.0 jit_solution(13746402277577572970)
XLA Ops:
  0.6 45.3 %interval.1 = (f32[10,16,2048]{2,1,0:T(8,128)S(1)}, f32[2,80,256]{2,1,0:T(8,128)S(1)}, f32[1,256]{1,0:T(1,128)S(1)}) custom-call(f32[10,16,2048]{2,1,0:T(8,128)} %atm.1, s32[3,2048]{1,0:T(4,128)} %offs.1, f32[3,2048]{1,0:T(4,128)} %edge.1, f32[10]{0:T(128)} %rates.1, f32[10,10]{1,0:T(8,128)} %mixing.1, s32[1,256]{1,0:T(1,128)} %bitcast.3, ...), custom_call_target="tpu_custom_call" | custom-call | tf_op jit(solution)/shard_map/interval/pallas_call | solution.py:591
  45.9 1.1 %store.1 = (f32[10,16,2048]{2,1,0:T(8,128)}, f32[2,80,256]{2,1,0:T(8,128)}, f32[1,256]{1,0:T(1,128)}) custom-call(f32[10,16,2048]{2,1,0:T(8,128)S(1)} %get-tuple-element.9.a, f32[2,80,256]{2,1,0:T(8,128)S(1)} %get-tuple-element.10.b, f32[1,256]{1,0:T(1,128)S(1)} %get-tuple-element.11.c), custom_call_target="tpu_custom_call" | custom-call | tf_op jit(solution)/shard_map/store/pallas_call | solution.py:645

commit v6 on v5

--- a/solution.py
+++ b/solution.py
@@ -53,44 +53,6 @@
     def level_of(step):
         return lax.rem(lev + step + n_lev, n_lev)
 
-    barrier = pltpu.get_barrier_semaphore()
-
-    def greet(where):
-        pl.semaphore_signal(barrier, inc=1, device_id=where, device_id_type=MESH)
-
-    first_opens = (sec > 0).astype(jnp.int32)
-    last_opens = (sec == n_sec - 1).astype(jnp.int32) if n_sec > 1 else jnp.int32(0)
-
-    def opens(p):
-        return ((p == 0) & (first_opens == 1)) | ((p == n_patch - 1) & (last_opens == 1))
-
-    opener = opens(patch)
-    openers_beside = first_opens * last_opens
-    expected = (n_lev - 1) + jnp.where(opener, openers_beside, n_patch - 1)
-    for side in range(2):
-        s, p, lower, higher = beside(side)
-        same = jnp.logical_not(lower | higher)
-
-        @pl.when(higher | (same & (opener | jnp.logical_not(opens(p)))))
-        def _(s=s, p=p):
-            for step in (-1, 0, 1):
-                greet((s, p, level_of(step)))
-
-        expected = expected + jnp.where(lower | (same & jnp.logical_not(opener)), 3, 0)
-    for i in range(1, n_lev):
-        greet((sec, patch, level_of(i)))
-
-    def greet_patch(i, carry):
-        other = lax.rem(patch + i, n_patch)
-
-        @pl.when(opener | jnp.logical_not(opens(other)))
-        def _():
-            greet((sec, other, lev))
-
-        return carry
-
-    lax.fori_loop(1, n_patch, greet_patch, 0)
-
     small = [
         (offs, offs_v), (edge, edge_v), (rates, rates_s), (owners, owners_v),
         (mixing, mix_v), (forcing_mix, fmix_v), (mask, mask_v), (ocean, ocean_v), (weights, weights_v),
@@ -104,6 +66,45 @@
     ]
     for load in atm_loads:
         load.start()
+
+    barrier = pltpu.get_barrier_semaphore()
+
+    def greet(where):
+        pl.semaphore_signal(barrier, inc=1, device_id=where, device_id_type=MESH)
+
+    first_opens = (sec > 0).astype(jnp.int32)
+    last_opens = (sec == n_sec - 1).astype(jnp.int32) if n_sec > 1 else jnp.int32(0)
+
+    def opens(p):
+        return ((p == 0) & (first_opens == 1)) | ((p == n_patch - 1) & (last_opens == 1))
+
+    opener = opens(patch)
+    openers_beside = first_opens * last_opens
+    expected = (n_lev - 1) + jnp.where(opener, openers_beside, n_patch - 1)
+    for side in range(2):
+        s, p, lower, higher = beside(side)
+        same = jnp.logical_not(lower | higher)
+
+        @pl.when(higher | (same & (opener | jnp.logical_not(opens(p)))))
+        def _(s=s, p=p):
+            for step in (-1, 0, 1):
+                greet((s, p, level_of(step)))
+
+        expected = expected + jnp.where(lower | (same & jnp.logical_not(opener)), 3, 0)
+    for i in range(1, n_lev):
+        greet((sec, patch, level_of(i)))
+
+    def greet_patch(i, carry):
+        other = lax.rem(patch + i, n_patch)
+
+        @pl.when(opener | jnp.logical_not(opens(other)))
+        def _():
+            greet((sec, other, lev))
+
+        return carry
+
+    lax.fori_loop(1, n_patch, greet_patch, 0)
+
     for load in loads[2:]:
         load.start()
 
@@ -155,10 +156,15 @@
 
     def send_edge(side):
         s, p, _, _ = beside(side)
-        for step in (0, -1, 1):
+        away, there = edge_send.at[side], edge_recv.at[1 - side]
+        for step, src, dst in (
+            (0, away, there.at[0:3]),
+            (1, away.at[1], there.at[3]),
+            (-1, away.at[0], there.at[4]),
+        ):
             pltpu.make_async_remote_copy(
-                src_ref=edge_send.at[side],
-                dst_ref=edge_recv.at[1 - side, 1 - step],
+                src_ref=src,
+                dst_ref=dst,
                 send_sem=edge_sem.at[0],
                 recv_sem=edge_sem.at[2 - side],
                 device_id=(s, p, level_of(step)),
@@ -370,21 +376,17 @@
         here = edge_recv.at[side]
         pltpu.make_async_copy(here, here, edge_sem.at[1 + side]).wait()
 
-        @pl.when(beside(side)[3])
-        def _():
-            send_edge(side)
-
         theirs = (in_group < HALO * (1 - side)) | (in_group >= GROUP - HALO * side)
-        corner = jnp.where(row < HALO, edge_recv[side, 2, 0], edge_recv[side, 0, 1])
+        corner = jnp.where(row < HALO, edge_recv[side, 4], edge_recv[side, 3])
         x = jnp.concatenate(
             [
-                jnp.where(theirs, edge_recv[side, 1, 0], own_edge[side, 0]),
-                jnp.where(theirs, edge_recv[side, 1, 1], own_edge[side, 1]),
+                jnp.where(theirs, edge_recv[side, 0], own_edge[side, 0]),
+                jnp.where(theirs, edge_recv[side, 1], own_edge[side, 1]),
                 jnp.where(inside_halo, jnp.where(theirs, corner, own_edge[side, 2]), 0.0),
             ],
             axis=0,
         )
-        factors = jnp.where(theirs, edge_recv[side, 1, 2], own_edge[side, 3])
+        factors = jnp.where(theirs, edge_recv[side, 2], own_edge[side, 3])
         sides = [factors[k : k + 1, :] for k in range(4)]
         centre = 1.0 - (sides[0] + sides[1] + sides[2] + sides[3]) - lane_vertical
         for last in (False, True):
@@ -404,6 +406,11 @@
             values = jnp.where(changed, pltpu.roll(values, first_lane, 1), 0.0)
             sums[d, half] = jnp.where(changed[: t1 - t0], values[: t1 - t0], sums[d, half])
         send_sums(d)
+
+        @pl.when(beside(side)[3])
+        def _():
+            send_edge(side)
+
         return carry
 
     lax.fori_loop(0, 2, one_side, 0)
@@ -612,7 +619,7 @@
                 vmem(ocean.shape, F32),
                 vmem(forcing_mix.shape, F32),
                 vmem((2, 3, 8, LANES), F32),
-                vmem((2, 3, 3, 8, LANES), F32),
+                vmem((2, 5, 8, LANES), F32),
                 vmem((2, 4, 8, LANES), F32),
                 vmem((2, klev, LANES), F32),
                 vmem((n_lev, block // LANES, 8, LANES), F32),

time: 47.2 us -> 45.6 us (0.966)
  Pallas kernels: 46.4 us -> 44.8 us
    pallas_call x1, Pallas kernels: 45.3 us -> 43.7 us  [per_device(): pl.pallas_call(functools.partial(interval, dims), out_shape=(jax.ShapeDty...]
where the time goes in v6:
time: 45.6 us; the launch traced here: 45.4 us
  Pallas kernels  44.8 us (98%)
  between operations  0.64 us (1%)
    pallas_call x1, Pallas kernels, per_device(): pl.pallas_call(functools.partial(interval, dims), out_shape=(jax.ShapeDty...  43.7 us
    pallas_call x1, Pallas kernels, per_device(): pl.pallas_call(store, out_shape=tuple((jax.ShapeDtypeStruct(x.shape, F32)...  1.13 us

profile of v6, /device:TPU:8, one launch (start us, length us, event | category | flops | bytes accessed | tf_op | source)
XLA Modules:
  0.0 45.4 jit_solution(2129403827908475383)
XLA Ops:
  0.6 43.7 %interval.1 = (f32[10,16,2048]{2,1,0:T(8,128)S(1)}, f32[2,80,256]{2,1,0:T(8,128)S(1)}, f32[1,256]{1,0:T(1,128)S(1)}) custom-call(f32[10,16,2048]{2,1,0:T(8,128)} %atm.1, s32[3,2048]{1,0:T(4,128)} %offs.1, f32[3,2048]{1,0:T(4,128)} %edge.1, f32[10]{0:T(128)} %rates.1, f32[10,10]{1,0:T(8,128)} %mixing.1, s32[1,256]{1,0:T(1,128)} %bitcast.3, ...), custom_call_target="tpu_custom_call" | custom-call | tf_op jit(solution)/shard_map/interval/pallas_call | solution.py:598
  44.3 1.1 %store.1 = (f32[10,16,2048]{2,1,0:T(8,128)}, f32[2,80,256]{2,1,0:T(8,128)}, f32[1,256]{1,0:T(1,128)}) custom-call(f32[10,16,2048]{2,1,0:T(8,128)S(1)} %get-tuple-element.9.a, f32[2,80,256]{2,1,0:T(8,128)S(1)} %get-tuple-element.10.b, f32[1,256]{1,0:T(1,128)S(1)} %get-tuple-element.11.c), custom_call_target="tpu_custom_call" | custom-call | tf_op jit(solution)/shard_map/store/pallas_call | solution.py:652

commit v7 on v6

--- a/solution.py
+++ b/solution.py
@@ -27,7 +27,7 @@
     ring, step1, coef, offs_v, edge_v, rates_s, mix_v, owners_v, weights_v, mask_v, ocean_v, base_v, fmix_v,
     edge_send, edge_recv, own_edge, outer_v, sums_a, sums_b, got_a, got_b, flux_send, flux_recv, back_send, back_recv,
     cols_hot, slot_hot, mix_cols,
-    atm_sem, in_sem, edge_sem, answer_sem, lev_send_sem, lev_up_sem, lev_down_sem, sum_sem, flux_sem, back_sem,
+    atm_sem, border_sem, in_sem, edge_sem, answer_sem, lev_send_sem, lev_up_sem, lev_down_sem, sum_sem, flux_sem, back_sem,
 ):
     n_sec, n_patch, n_lev = dims
     ntr, klev, ncol = atm.shape
@@ -60,11 +60,19 @@
     loads = [pltpu.make_async_copy(a, b, in_sem.at[i]) for i, (a, b) in enumerate(small)]
     for i in (0, 1):
         loads[i].start()
+    border_loads = [
+        pltpu.make_async_copy(
+            atm.at[:, :, at : at + LANES], ring.at[:, 0:klev, LANES + at : 2 * LANES + at], border_sem.at[i]
+        )
+        for i, at in enumerate((0, ncol - LANES))
+    ]
     atm_loads = [
-        pltpu.make_async_copy(atm.at[t], ring.at[t, 0:klev, LANES : LANES + ncol], atm_sem.at[t])
+        pltpu.make_async_copy(
+            atm.at[t, :, LANES : ncol - LANES], ring.at[t, 0:klev, 2 * LANES : ncol], atm_sem.at[t]
+        )
         for t in range(ntr)
     ]
-    for load in atm_loads:
+    for load in border_loads + atm_loads:
         load.start()
 
     barrier = pltpu.get_barrier_semaphore()
@@ -97,13 +105,20 @@
     def greet_patch(i, carry):
         other = lax.rem(patch + i, n_patch)
 
-        @pl.when(opener | jnp.logical_not(opens(other)))
+        @pl.when(jnp.logical_not(opens(other)))
         def _():
             greet((sec, other, lev))
 
         return carry
 
-    lax.fori_loop(1, n_patch, greet_patch, 0)
+    for p in (0, n_patch - 1):
+        @pl.when(opener & opens(jnp.int32(p)) & (patch != p))
+        def _(p=p):
+            greet((sec, p, lev))
+
+    @pl.when(jnp.logical_not(opener))
+    def _():
+        lax.fori_loop(1, n_patch, greet_patch, 0)
 
     for load in loads[2:]:
         load.start()
@@ -120,7 +135,7 @@
 
     lane = lax.broadcasted_iota(jnp.int32, (8, LANES), 1)
     row = lax.broadcasted_iota(jnp.int32, (8, LANES), 0)
-    for load in atm_loads:
+    for load in border_loads:
         load.wait()
 
     def packed(of_tracer, source, width, target):
@@ -187,6 +202,10 @@
             for step in (-1, 0, 1):
                 answer((s, p, level_of(step)))
 
+    @pl.when(opener)
+    def _():
+        lax.fori_loop(1, n_patch, greet_patch, 0)
+
     for p in (0, n_patch - 1):
         @pl.when(jnp.logical_not(opener) & opens(jnp.int32(p)))
         def _(p=p):
@@ -230,7 +249,7 @@
     def _():
         ring[:, klev : klev + HALO, LANES : LANES + ncol] = jnp.zeros((ntr, HALO, ncol), F32)
 
-    for load in loads[2:]:
+    for load in loads[2:] + atm_loads:
         load.wait()
     owned = owners_v[...]
     hot = (lax.broadcasted_iota(jnp.int32, (n_patch, block), 0) == owned).astype(F32)
@@ -570,7 +589,8 @@
 
 
 def store(a, b, c, a_out, b_out, c_out, sem):
-    copies = [pltpu.make_async_copy(x, y, sem.at[i]) for i, (x, y) in enumerate(((a, a_out), (b, b_out), (c, c_out)))]
+    pairs = [(a.at[t], a_out.at[t]) for t in range(a.shape[0])] + [(b, b_out), (c, c_out)]
+    copies = [pltpu.make_async_copy(x, y, sem.at[i]) for i, (x, y) in enumerate(pairs)]
     for copy in copies:
         copy.start()
     for copy in copies:
@@ -634,6 +654,7 @@
                 vmem((LANES, block), BF16),
                 vmem((ntr, nflux, block), F32),
                 dma((ntr,)),
+                dma((2,)),
                 dma((9,)),
                 dma((3,)),
                 pltpu.SemaphoreType.REGULAR,
@@ -654,7 +675,7 @@
             out_shape=tuple(jax.ShapeDtypeStruct(x.shape, F32) for x in out),
             in_specs=[in_vmem] * 3,
             out_specs=(any_space,) * 3,
-            scratch_shapes=[dma((3,))],
+            scratch_shapes=[dma((ntr + 2,))],
             compiler_params=pltpu.CompilerParams(vmem_limit_bytes=8 * 1024 * 1024),
             name="store",
         )(*out)

time: 45.6 us -> 45.7 us (level)
  no operation moved by 1% of the time
where the time goes in v7:
time: 45.7 us; the launch traced here: 45.5 us
  Pallas kernels  44.9 us (98%)
  between operations  0.64 us (1%)
    pallas_call x1, Pallas kernels, per_device(): pl.pallas_call(functools.partial(interval, dims), out_shape=(jax.ShapeDty...  43.7 us
    pallas_call x1, Pallas kernels, per_device(): pl.pallas_call(store, out_shape=tuple((jax.ShapeDtypeStruct(x.shape, F32)...  1.21 us

profile of v7, /device:TPU:8, one launch (start us, length us, event | category | flops | bytes accessed | tf_op | source)
XLA Modules:
  0.0 45.5 jit_solution(966806632408116538)
XLA Ops:
  0.6 43.7 %interval.1 = (f32[10,16,2048]{2,1,0:T(8,128)S(1)}, f32[2,80,256]{2,1,0:T(8,128)S(1)}, f32[1,256]{1,0:T(1,128)S(1)}) custom-call(f32[10,16,2048]{2,1,0:T(8,128)} %atm.1, s32[3,2048]{1,0:T(4,128)} %offs.1, f32[3,2048]{1,0:T(4,128)} %edge.1, f32[10]{0:T(128)} %rates.1, f32[10,10]{1,0:T(8,128)} %mixing.1, s32[1,256]{1,0:T(1,128)} %bitcast.3, ...), custom_call_target="tpu_custom_call" | custom-call | tf_op jit(solution)/shard_map/interval/pallas_call | solution.py:618
  44.3 1.2 %store.1 = (f32[10,16,2048]{2,1,0:T(8,128)}, f32[2,80,256]{2,1,0:T(8,128)}, f32[1,256]{1,0:T(1,128)}) custom-call(f32[10,16,2048]{2,1,0:T(8,128)S(1)} %get-tuple-element.9.a, f32[2,80,256]{2,1,0:T(8,128)S(1)} %get-tuple-element.10.b, f32[1,256]{1,0:T(1,128)S(1)} %get-tuple-element.11.c), custom_call_target="tpu_custom_call" | custom-call | tf_op jit(solution)/shard_map/store/pallas_call | solution.py:673
